TPU v7x, 1024 devices: a whole 4x8x16 slice. The times are simulated.
1024 devices in a mesh: op: 4 (over x), vp: 16 (over z), cd: 16 (over y, core).
Axes of the slice: x: 4, y: 8, z: 16, core: 2. Of those that a mesh axis runs over, the one named last changes fastest.
Arguments:
- t2_amps: float32 [1024, 65536], P(('op', 'vp'), 'cd'), may hold values from -16 to 16
- w_slab: float32 [16384, 32768], P('vp', 'cd'), may hold values from -0.0625 to 0.0625
- irrep_ab: int32 [16384], replicated, may hold values from 0 to 7, as said below
- irrep_cd: int32 [65536], P('cd'), may hold values from 0 to 7, as said below
Outputs:
- ladder: float32 [1024, 16384], P(('op', 'cd'), 'vp')
Inputs may be any that keep to these rules, and one draw needn't show every extreme that they name: `irrep_ab`: within the rows of each owner (aligned blocks of 1024) nondecreasing and taking exactly two consecutive values. `irrep_cd`: within each aligned block of 4096 nondecreasing and taking every value; each value on at most 1024 entries of a block, and in every block two consecutive values have exactly 1024 entries each.
All inputs are finite; a program needn't handle non-finite values.
Results may differ from a plain program's by a relative error of at most 0.0003.
Values sent between devices are 32-bit elements; how exact they have to be, the bound alone decides.
No kernel may reach another device: no remote copies, remote signals or barrier semaphores. Data moves between devices by JAX's collectives and lax.ppermute only.
A program may use at most 32 MiB of HBM per device.

v0:
```python
import jax
import jax.numpy as jnp
from jax import lax
from jax.sharding import PartitionSpec as P


def contract(amps, masked):
    return lax.dot_general(
        amps,
        masked,
        (((1,), (1,)), ((), ())),
        precision=lax.Precision.HIGHEST,
        preferred_element_type=jnp.float32,
    )


def per_device(t2_amps, w_slab, irrep_ab, irrep_cd):
    owners = lax.axis_size("vp")
    ab_dev = w_slab.shape[0]
    width = w_slab.shape[1]
    cd_dev = irrep_cd.shape[0]
    lows = irrep_ab.reshape(owners, ab_dev)[:, 0]
    counts = jnp.sum((irrep_cd[None, :] < lows[:, None]).astype(jnp.int32), axis=1)
    starts = jnp.minimum(counts, cd_dev - width)
    own = lax.axis_index("vp")
    own_start = starts[own]
    own_labels = lax.dynamic_slice_in_dim(irrep_ab, own * ab_dev, ab_dev, 0)
    col_labels = lax.dynamic_slice_in_dim(irrep_cd, own_start, width, 0)
    masked = jnp.where(own_labels[:, None] == col_labels[None, :], w_slab, jnp.zeros_like(w_slab))
    amps_group = lax.dynamic_slice_in_dim(
        lax.all_gather(t2_amps, "vp", axis=0, tiled=True), own_start, width, 1
    )
    share = amps_group.shape[0] // lax.axis_size("cd")
    partial_rows = contract(amps_group, masked)
    total = lax.psum(partial_rows, "cd")
    return lax.dynamic_slice_in_dim(total, lax.axis_index("cd") * share, share, 0)


def solution(mesh):
    placed = (P(("op", "vp"), "cd"), P("vp", "cd"), P(), P("cd"))
    return jax.shard_map(
        per_device, mesh=mesh, in_specs=placed, out_specs=P(("op", "cd"), "vp"), check_vma=False
    )
```

profile of v0, /device:TPU:1, one launch (start us, length us, event | category | flops | bytes accessed | tf_op | source)
XLA Modules:
  0.0 245.0 jit_solution(898187291116825174)
XLA Ops:
  6.5 0.0 all-gather.2.cloned.1.call-start
  6.5 0.7 all-gather.2.cloned.1.call-update
  7.3 0.0 all-reduce.2.cloned.1.call-start
  7.3 0.9 reshape.6
  8.2 0.7 dynamic_slice.17
  8.9 0.1 slice_reduce_fusion
  9.0 0.9 convert_reduce_fusion
  9.9 0.6 dynamic_slice.15
  12.5 0.8 dynamic_slice.18
  13.2 79.5 %all-gather.2.cloned.1.call-done = f32[256,4096]{1,0:T(8,128)} async-done(((f32[16,4096]{1,0:T(8,128)}), f32[256,4096]{1,0:T(8,128)}) %all-gather.2.cloned.1.call-update) | async-done | bytes 4194320 | tf_op jit(solution)/shard_map/all_gather | solution.py:31
  92.7 12.0 %fusion = f32[256,1024]{1,0:T(8,128)} fusion(f32[1024,2048]{1,0:T(8,128)} %param.5, s32[2048]{0:T(1024)S(1)} %dynamic_slice.18, s32[1024]{0:T(1024)S(1)} %dynamic_slice.17, f32[256,4096]{1,0:T(8,128)} %all-gather.2.cloned.1.call-done, s32[]{:T(128)S(6)} %select_n.18), kind=kOutput, calls=%fused_computation | convolution fusion | flops 6446645248 | bytes 11546628 | tf_op jit(solution)/shard_map/dot_general | solution.py:8
  104.7 0.0 all-reduce.2.cloned.1.call-update
  104.7 132.0 %all-reduce.2.cloned.1.call-done = f32[256,1024]{1,0:T(8,128)} async-done(((f32[256,1024]{1,0:T(8,128)}), f32[256,1024]{1,0:T(8,128)}) %all-reduce.2.cloned.1.call-update) | async-done | bytes 1048592 | tf_op jit(solution)/shard_map/psum | solution.py:35
  236.7 1.5 constant_dynamic-slice_fusion
  (1 shorter events, 0.0 us)
Async XLA Ops:
  6.5 86.2 %all-gather.2.cloned.1.call-start = ((), (), s32[]{:S(2)}) async-start(), calls=%async_computation | async-start | bytes 4456448 | tf_op jit(solution)/shard_map/all_gather | solution.py:31
  7.3 229.4 %all-reduce.2.cloned.1.call-start = ((), (), s32[]{:S(2)}) async-start(), calls=%async_computation.1 | async-start | bytes 2097152 | tf_op jit(solution)/shard_map/psum | solution.py:35
Sparse Core Ops, SparseCore 0:
  10.0 82.6 all-gather.1
  104.9 131.7 all-reduce.1
where the time goes:
time: 245 us
  waiting for transfers between devices  212 us (87%)
  between operations  15.4 us (6%)
  matrix products  12 us (5%)
  local copies, waits for them, and re-layouts  4.51 us (2%)
    psum x1, waiting for transfers between devices, per_device(): total = lax.psum(partial_rows, 'cd')  132 us
    all_gather x1, waiting for transfers between devices, per_device(): lax.all_gather(t2_amps, 'vp', axis=0, tiled=True)  79.5 us
    dot_general x1, matrix products, contract(): lax.dot_general(amps, masked, (((1,), (1,)), ((), ())), precision=lax.Pre...  12 us
  transfers between devices with their start and end apart: 2, of which 2 were waited for; matrix products, arithmetic and copies ran while one was open for 2% of the time, Pallas kernels for 0%

commit v1 on v0

v1 whole, which is shorter than its diff:
```python
import jax
import jax.numpy as jnp
from jax import lax
from jax.sharding import PartitionSpec as P


def contract(amps, masked):
    return lax.dot_general(
        amps,
        masked,
        (((1,), (1,)), ((), ())),
        precision=lax.Precision.HIGH,
        preferred_element_type=jnp.float32,
    )


def reduce_rows(partial_rows):
    n_cd = lax.axis_size("cd")
    rows, cols = partial_rows.shape
    share = rows // n_cd
    core = lax.axis_index("cd") % 2
    blocks = partial_rows.reshape(n_cd // 2, 2, share, cols)
    mine = lax.dynamic_index_in_dim(blocks, core, 1, keepdims=False)
    other = lax.dynamic_index_in_dim(blocks, 1 - core, 1, keepdims=False)
    pair = [(i, i ^ 1) for i in range(n_cd)]
    both = mine + lax.ppermute(other, "cd", pair)
    groups = [[c for c in range(n_cd) if c % 2 == p] for p in range(2)]
    parts = lax.all_to_all(both, "cd", 0, 0, axis_index_groups=groups)
    return jnp.sum(parts, axis=0)


def per_device(t2_amps, w_slab, irrep_ab, irrep_cd):
    ab_dev = w_slab.shape[0]
    width = w_slab.shape[1]
    cd_dev = irrep_cd.shape[0]
    own = lax.axis_index("vp")
    own_labels = lax.dynamic_slice_in_dim(irrep_ab, own * ab_dev, ab_dev, 0)
    count = jnp.sum((irrep_cd < own_labels[0]).astype(jnp.int32))
    own_start = jnp.minimum(count, cd_dev - width)
    col_labels = lax.dynamic_slice_in_dim(irrep_cd, own_start, width, 0)
    masked = jnp.where(own_labels[:, None] == col_labels[None, :], w_slab, jnp.zeros_like(w_slab))
    amps_group = lax.dynamic_slice_in_dim(
        lax.all_gather(t2_amps, "vp", axis=0, tiled=True), own_start, width, 1
    )
    return reduce_rows(contract(amps_group, masked))


def solution(mesh):
    placed = (P(("op", "vp"), "cd"), P("vp", "cd"), P(), P("cd"))
    return jax.shard_map(
        per_device, mesh=mesh, in_specs=placed, out_specs=P(("op", "cd"), "vp"), check_vma=False
    )
```

time: 245 us -> 144 us (0.59)
  waiting for transfers between devices: 212 us -> 83 us
  blocking collectives: 0 us -> 22.9 us
  starting transfers between devices: 0.04 us -> 11 us
  matrix products: 12 us -> 7.42 us
  local copies, waits for them, and re-layouts: 4.51 us -> 2.04 us
    psum x1 -> x0, waiting for transfers between devices: 132 us -> none  [per_device(): total = lax.psum(partial_rows, 'cd')]
    all_to_all x0 -> x1, blocking collectives: none -> 22.9 us  [reduce_rows(): parts = lax.all_to_all(both, 'cd', 0, 0, axis_index_groups=groups)]
    ppermute x0 -> x1, starting transfers between devices: none -> 11 us  [reduce_rows(): both = mine + lax.ppermute(other, 'cd', pair)]
    dot_general x1, matrix products: 12 us -> 7.42 us  [contract(): lax.dot_general(amps, masked, (((1,), (1,)), ((), ())), precision=lax.Pre...]
  transfers between devices with their start and end apart: 2 -> 2, of which waited for: 2 -> 2; matrix products, arithmetic and copies ran while one was open for 2% -> 3% of each run, Pallas kernels for 0% -> 0%
where the time goes in v1:
time: 144 us; the launch traced here: 143 us
  waiting for transfers between devices  83 us (58%)
  blocking collectives  22.9 us (16%)
  between operations  14.1 us (10%)
  starting transfers between devices  11 us (8%)
  matrix products  7.42 us (5%)
  other arithmetic  2.74 us (2%)
  local copies, waits for them, and re-layouts  2.04 us (1%)
    all_gather x1, waiting for transfers between devices, per_device(): lax.all_gather(t2_amps, 'vp', axis=0, tiled=True)  80.8 us
    all_to_all x1, blocking collectives, reduce_rows(): parts = lax.all_to_all(both, 'cd', 0, 0, axis_index_groups=groups)  22.9 us
    ppermute x1, starting transfers between devices, reduce_rows(): both = mine + lax.ppermute(other, 'cd', pair)  11 us
    dot_general x1, matrix products, contract(): lax.dot_general(amps, masked, (((1,), (1,)), ((), ())), precision=lax.Pre...  7.42 us
  transfers between devices with their start and end apart: 2, of which 2 were waited for; matrix products, arithmetic and copies ran while one was open for 3% of the time, Pallas kernels for 0%

profile of v1, /device:TPU:1, one launch (start us, length us, event | category | flops | bytes accessed | tf_op | source)
XLA Modules:
  0.0 143.3 jit_solution(13862958073475554755)
XLA Ops:
  6.5 0.0 all-gather.2.cloned.1.call-start
  6.5 0.7 all-gather.2.cloned.1.call-update
  7.3 0.7 dynamic_slice.16
  8.0 0.5 slice.3
  8.5 2.0 %convert_reduce_fusion = s32[]{:T(128)} fusion(s32[4096]{0:T(1024)} %param.7, s32[]{:T(128)} %bitcast), kind=kLoop, calls=%fused_computation.9 | loop fusion | flops 12287 | bytes 16392 | tf_op jit(solution)/shard_map/reduce_sum | solution.py:38
  11.1 0.8 dynamic_slice.18
  11.9 80.8 %all-gather.2.cloned.1.call-done = f32[256,4096]{1,0:T(8,128)} async-done(((f32[16,4096]{1,0:T(8,128)}), f32[256,4096]{1,0:T(8,128)}) %all-gather.2.cloned.1.call-update) | async-done | bytes 4194320 | tf_op jit(solution)/shard_map/all_gather | solution.py:43
  92.7 7.4 %fusion = f32[256,1024]{1,0:T(8,128)S(1)} fusion(f32[1024,2048]{1,0:T(8,128)} %param.5, s32[2048]{0:T(1024)S(1)} %dynamic_slice.18, s32[1024]{0:T(1024)S(1)} %dynamic_slice.16, f32[256,4096]{1,0:T(8,128)} %all-gather.2.cloned.1.call-done, s32[]{:T(128)S(6)} %select_n.26), kind=kOutput, calls=%fused_computation | convolution fusion | flops 3225419776 | bytes 11546628 | tf_op jit(solution)/shard_map/dot_general | solution.py:8
  100.2 11.0 %collective-permute-start = (f32[8,16,1024]{2,1,0:T(8,128)S(1)}, f32[8,16,1024]{2,1,0:T(8,128)S(1)}, u32[]{:S(2)}, u32[]{:S(2)}) collective-permute-start(f32[8,16,1024]{2,1,0:T(8,128)S(1)} %dynamic-slice_bitcast_fusion), channel_id=1, source_target_pairs={{0,1},{1,0},{2,3},{3,2},{4,5},{5,4},{6,7},{7,6},{8,9},{9,8},{10,11... | collective-permute-start | bytes 1572872 | tf_op jit(solution)/shard_map/ppermute | solution.py:26
  111.3 1.5 %collective-permute-done = f32[8,16,1024]{2,1,0:T(8,128)S(1)} collective-permute-done((f32[8,16,1024]{2,1,0:T(8,128)S(1)}, f32[8,16,1024]{2,1,0:T(8,128)S(1)}, u32[]{:S(2)}, u32[]{:S(2)}) %collective-permute-start) | collective-permute-done | bytes 524320 | tf_op jit(solution)/shard_map/ppermute | solution.py:26
  112.8 0.1 bitcast_add_fusion
  112.8 22.9 %all_to_all.5 = f32[8,16,1024]{2,1,0:T(8,128)S(1)} all-to-all(f32[8,16,1024]{2,1,0:T(8,128)S(1)} %bitcast_add_fusion), channel_id=1, replica_groups={{0,2,4,6,8,10,12,14},{1,3,5,7,9,11,13,15},{16,18,20,22,24,26,28,30},{17..., dimensions={0} | all-to-all | bytes 1048576 | tf_op jit(solution)/shard_map/all_to_all | solution.py:28
  135.8 0.7 reduce_sum.19
  (1 shorter events, 0.0 us)
Async XLA Ops:
  6.5 86.2 %all-gather.2.cloned.1.call-start = ((), (), s32[]{:S(2)}) async-start(), calls=%async_computation.1 | async-start | bytes 4456448 | tf_op jit(solution)/shard_map/all_gather | solution.py:43
  100.2 12.6 %collective-permute-start = (f32[8,16,1024]{2,1,0:T(8,128)S(1)}, f32[8,16,1024]{2,1,0:T(8,128)S(1)}, u32[]{:S(2)}, u32[]{:S(2)}) collective-permute-start(f32[8,16,1024]{2,1,0:T(8,128)S(1)} %dynamic-slice_bitcast_fusion), channel_id=1, source_target_pairs={{0,1},{1,0},{2,3},{3,2},{4,5},{5,4},{6,7},{7,6},{8,9},{9,8},{10,11... | collective-permute-start | bytes 1572872 | tf_op jit(solution)/shard_map/ppermute | solution.py:26
Sparse Core Ops, SparseCore 0:
  10.0 82.6 all-gather.1

commit v2 on v1

v2 whole, which is shorter than its diff:
```python
import functools

import jax
import jax.numpy as jnp
from jax import lax
from jax.experimental import pallas as pl
from jax.experimental.pallas import tpu as pltpu
from jax.sharding import PartitionSpec as P

LANES = 128
AB_TILE = 256


def contract_kernel(rels, shapes, width, carried, scal, *refs):
    n_src = len(shapes)
    srcs, refs = refs[:n_src], refs[n_src:]
    w_ref, refs = refs[0], refs[1:]
    if carried:
        old_mine, old_other, refs = refs[0], refs[1], refs[2:]
    mine, other, hi, lo = refs
    tile0, off, n_low, a0, a1, a2, z, d, core = [scal[i] for i in range(9)]
    step = pl.program_id(0)
    tiles = width // LANES
    share = hi.shape[0] // len(rels)

    @pl.when(step == 0)
    def build():
        lane = lax.broadcasted_iota(jnp.int32, (share, LANES), 1)
        keep = lane < LANES - off
        turn = lax.rem(LANES - off, LANES)
        row = 0
        for ref, count in zip(srcs, shapes):
            for i in range(1 if count is None else count):
                rolled = None
                for j in range(tiles + 1):
                    if count is None:
                        piece = ref[:, pl.ds(tile0 + j, 1)]
                    else:
                        piece = ref[i, :, pl.ds(j, 1)]
                    piece = piece.reshape(share, LANES)
                    new = pltpu.roll(piece, turn, 1)
                    if rolled is not None:
                        value = jnp.where(keep, rolled, new)
                        high = value.astype(jnp.bfloat16)
                        rest = (value - high.astype(jnp.float32)).astype(jnp.bfloat16)
                        at = (slice(row, row + share), slice((j - 1) * LANES, j * LANES))
                        hi[at] = high
                        lo[at] = rest
                    rolled = new
                row += share

    rows = lax.broadcasted_iota(jnp.int32, (AB_TILE, 1), 0) + step * AB_TILE
    first = jnp.where(rows < n_low, a0, a1)
    last = jnp.where(rows < n_low, a1, a2)
    cols = lax.broadcasted_iota(jnp.int32, (AB_TILE, width), 1)
    w = jnp.where((cols >= first) & (cols < last), w_ref[...], 0.0)
    w_hi = w.astype(jnp.bfloat16)
    w_lo = (w - w_hi.astype(jnp.float32)).astype(jnp.bfloat16)
    dot = functools.partial(
        lax.dot_general,
        dimension_numbers=(((1,), (1,)), ((), ())),
        preferred_element_type=jnp.float32,
    )
    out = dot(hi[...], w_lo) + dot(lo[...], w_hi) + dot(hi[...], w_hi)
    if carried:
        mine[...] = old_mine[...]
        other[...] = old_other[...]
    for i, rel in enumerate(rels):
        block = (z + rel * d + 32) & 15
        value = out[i * share : (i + 1) * share]

        @pl.when((block & 1) == core)
        def keep_block():
            mine[pl.ds(block >> 1, 1)] = value[None]

        @pl.when((block & 1) != core)
        def send_block():
            other[pl.ds(block >> 1, 1)] = value[None]


def contract(scal, sources, rels, w_slab, old=()):
    ab, width = w_slab.shape
    shapes = [None if s.ndim == 4 else s.shape[0] for s in sources]
    share = 16
    rows = share * len(rels)
    whole = [pl.BlockSpec(s.shape, functools.partial(lambda n, i: (0,) * n, s.ndim)) for s in sources]
    out_spec = pl.BlockSpec((8, share, AB_TILE), lambda i: (0, 0, i))
    out_shape = jax.ShapeDtypeStruct((8, share, ab), jnp.float32)
    return pl.pallas_call(
        functools.partial(contract_kernel, rels, shapes, width, bool(old)),
        grid=(ab // AB_TILE,),
        in_specs=[pl.BlockSpec(memory_space=pltpu.SMEM)]
        + whole
        + [pl.BlockSpec((AB_TILE, width), lambda i: (i, 0))]
        + [out_spec] * len(old),
        out_specs=[out_spec, out_spec],
        out_shape=[out_shape, out_shape],
        scratch_shapes=[pltpu.VMEM((rows, width), jnp.bfloat16)] * 2,
        compiler_params=pltpu.CompilerParams(vmem_limit_bytes=40 * 1024 * 1024),
        cost_estimate=pl.CostEstimate(
            flops=6 * rows * width * ab, bytes_accessed=4 * ab * width, transcendentals=0
        ),
    )(scal, *sources, w_slab, *old)


def reduce_rows(mine, other):
    n_cd = lax.axis_size("cd")
    pair = [(i, i ^ 1) for i in range(n_cd)]
    both = mine + lax.ppermute(other, "cd", pair)
    groups = [[c for c in range(n_cd) if c % 2 == p] for p in range(2)]
    parts = lax.all_to_all(both, "cd", 0, 0, axis_index_groups=groups)
    return jnp.sum(parts, axis=0)


def per_device(t2_amps, w_slab, irrep_ab, irrep_cd):
    n_vp = lax.axis_size("vp")
    n_cd = lax.axis_size("cd")
    ab_dev, width = w_slab.shape
    rows_dev, cd_dev = t2_amps.shape
    win_tiles = width // LANES + 1
    z = lax.axis_index("vp")
    c = lax.axis_index("cd")
    core = c % 2
    d = 1 - 2 * core

    def move(array, k):
        pairs = [
            (v * n_cd + e, ((v + (k if e % 2 == 0 else -k)) % n_vp) * n_cd + e)
            for v in range(n_vp)
            for e in range(n_cd)
        ]
        return lax.ppermute(array, ("vp", "cd"), pairs)

    labels = irrep_ab.reshape(n_vp, ab_dev)
    lows = labels[:, 0]
    counts = jnp.sum((irrep_cd[None, :] < lows[:, None]).astype(jnp.int32), axis=1)
    starts = jnp.minimum(counts, cd_dev - width)
    tile_of = jnp.minimum(starts // LANES, cd_dev // LANES - win_tiles)
    low = lows[z]
    start = starts[z]
    tile0 = tile_of[z]
    below1 = jnp.sum((irrep_cd <= low).astype(jnp.int32))
    below2 = jnp.sum((irrep_cd <= low + 1).astype(jnp.int32))
    n_low = jnp.sum((labels[z] == low).astype(jnp.int32))
    scal = jnp.stack(
        [tile0, start - tile0 * LANES, n_low, counts[z] - start, below1 - start, below2 - start, z, d, core]
    ).astype(jnp.int32)

    def window(block, k):
        at = tile_of[(z + k * d + 2 * n_vp) % n_vp]
        return lax.dynamic_slice(block, (0, at, 0, 0), (block.shape[0], win_tiles, 8, LANES))

    own = t2_amps.reshape(rows_dev // 8, 8, cd_dev // LANES, LANES).transpose(0, 2, 1, 3)
    x1 = move(own, 3)
    y1 = move(own, -3)
    x2 = move(x1, 3)
    y2 = move(y1, -3)
    near_x = move(jnp.stack([window(b, 1) for b in (own, x1, y1)]), 1)
    near_y = move(jnp.stack([window(b, -1) for b in (own, x1, y1)]), -1)
    far_x = move(jnp.stack([window(b, 1) for b in (x2, y2)]), 1)
    far_y = move(jnp.stack([window(b, -1) for b in (x2, y2)]), -1)
    edge = move(window(x2, 2)[None], 2)
    first = contract(
        scal,
        [own, x1, y1, x2, y2, near_x, near_y],
        [0, -3, 3, -6, 6, -1, -4, 2, 1, -2, 4],
        w_slab,
    )
    mine, other = contract(scal, [far_x, far_y, edge], [-7, 5, -5, 7, -8], w_slab, first)
    return reduce_rows(mine, other)


def solution(mesh):
    placed = (P(("op", "vp"), "cd"), P("vp", "cd"), P(), P("cd"))
    return jax.shard_map(
        per_device, mesh=mesh, in_specs=placed, out_specs=P(("op", "cd"), "vp"), check_vma=False
    )
```

time: 144 us -> 133 us (0.924)
  waiting for transfers between devices: 83 us -> 12.9 us
  starting transfers between devices: 11 us -> 50.6 us
  Pallas kernels: 0 us -> 15.3 us
  local copies, waits for them, and re-layouts: 2.04 us -> 10.2 us
  matrix products: 7.42 us -> 0 us
  other arithmetic: 2.74 us -> 6.52 us
  between operations: 14.1 us -> 11.5 us
  blocking collectives: 22.9 us -> 25.3 us
    all_gather x1 -> x0, waiting for transfers between devices: 80.8 us -> none  [per_device(): lax.all_gather(t2_amps, 'vp', axis=0, tiled=True)]
    ppermute x0 -> x9, starting transfers between devices: none -> 48.7 us  [move(): return lax.ppermute(array, ('vp', 'cd'), pairs)]
    pallas_call x0 -> x2, Pallas kernels: none -> 15.3 us  [contract(): pl.pallas_call(functools.partial(contract_kernel, rels, shapes, width, bo...]
    ppermute x0 -> x9, waiting for transfers between devices: none -> 11.1 us  [move(): return lax.ppermute(array, ('vp', 'cd'), pairs)]
    ppermute x1, starting transfers between devices: 11 us -> 1.92 us  [reduce_rows(): both = mine + lax.ppermute(other, 'cd', pair)]
    dot_general x1 -> x0, matrix products: 7.42 us -> none  [contract(): lax.dot_general(amps, masked, (((1,), (1,)), ((), ())), precision=lax.Pre...]
    unnamed x0 -> x6, local copies, waits for them, and re-layouts: none -> 4.33 us
    another operation x0 -> x5, local copies, waits for them, and re-layouts: none -> 2.43 us  [the longest x1 1.33 us: per_device(): jnp.stack([tile0, start - tile0 * LANES, n_low, counts[z] - start, below1...]
  transfers between devices with their start and end apart: 2 -> 10, of which waited for: 2 -> 4; matrix products, arithmetic and copies ran while one was open for 3% -> 9% of each run, Pallas kernels for 0% -> 6%
where the time goes in v2:
time: 133 us; the launch traced here: 132 us
  starting transfers between devices  50.6 us (38%)
  blocking collectives  25.3 us (19%)
  Pallas kernels  15.3 us (12%)
  waiting for transfers between devices  12.9 us (10%)
  between operations  11.5 us (9%)
  local copies, waits for them, and re-layouts  10.2 us (8%)
  other arithmetic  6.52 us (5%)
    ppermute x9, starting transfers between devices, move(): return lax.ppermute(array, ('vp', 'cd'), pairs)  48.7 us
    all_to_all x1, blocking collectives, reduce_rows(): parts = lax.all_to_all(both, 'cd', 0, 0, axis_index_groups=groups)  25.3 us
    pallas_call x2, Pallas kernels, contract(): pl.pallas_call(functools.partial(contract_kernel, rels, shapes, width, bo...  15.3 us
    ppermute x9, waiting for transfers between devices, move(): return lax.ppermute(array, ('vp', 'cd'), pairs)  11.1 us
    unnamed x6, local copies, waits for them, and re-layouts  4.33 us
  transfers between devices with their start and end apart: 10, of which 4 were waited for; matrix products, arithmetic and copies ran while one was open for 9% of the time, Pallas kernels for 6%

profile of v2, /device:TPU:1, one launch (start us, length us, event | category | flops | bytes accessed | tf_op | source)
XLA Modules:
  0.0 132.3 jit_solution(10113449565042986183)
XLA Ops:
  0.0 18.7 %collective-permute-start = (f32[2,32,8,128]{3,2,1,0:T(8,128)}, f32[2,32,8,128]{3,2,1,0:T(8,128)S(1)}, u32[]{:S(2)}, u32[]{:S(2)}) collective-permute-start(f32[2,32,8,128]{3,2,1,0:T(8,128)} %bitcast.44), channel_id=1, source_target_pairs={{0,48},{1,209},{2,50},{3,211},{4,52},{5,213},{6,54},{7,215},{8,56}... | collective-permute-start | bytes 786440 | tf_op jit(solution)/shard_map/ppermute | solution.py:132
  18.8 1.9 %collective-permute-start.2 = (f32[2,32,8,128]{3,2,1,0:T(8,128)}, f32[2,32,8,128]{3,2,1,0:T(8,128)S(1)}, u32[]{:S(2)}, u32[]{:S(2)}) collective-permute-start(f32[2,32,8,128]{3,2,1,0:T(8,128)} %bitcast.45), channel_id=1, source_target_pairs={{0,208},{1,49},{2,210},{3,51},{4,212},{5,53},{6,214},{7,55},{8,216... | collective-permute-start | bytes 786440 | tf_op jit(solution)/shard_map/ppermute | solution.py:132
  20.7 0.9 reshape.14
  21.5 0.1 fusion.2
  21.7 0.9 convert_reduce_fusion
  22.7 0.7 fusion.3
  25.7 0.6 dynamic_slice.69
  27.7 0.7 dynamic_slice.66
  28.3 0.5 constant_dynamic-slice_fusion
  32.6 1.0 dynamic-slice_bitcast_fusion.2
  33.6 1.4 %collective-permute-done.refs_1_ = f32[2,32,8,128]{3,2,1,0:T(8,128)S(1)} collective-permute-done((f32[2,32,8,128]{3,2,1,0:T(8,128)}, f32[2,32,8,128]{3,2,1,0:T(8,128)S(1)}, u32[]{:S(2)}, u32[]{:S(2)}) %collective-permute-start) | collective-permute-done | bytes 262176 | tf_op jit(solution)/shard_map/ppermute | solution.py:132
  35.0 7.1 %collective-permute-start.1 = (f32[2,32,8,128]{3,2,1,0:T(8,128)S(1)}, f32[2,32,8,128]{3,2,1,0:T(8,128)S(1)}, u32[]{:S(2)}, u32[]{:S(2)}) collective-permute-start(f32[2,32,8,128]{3,2,1,0:T(8,128)S(1)} %collective-permute-done.refs_1_), channel_id=1, source_target_pairs={{0,48},{1,209},{2,50},{3,211},{4,52},{5,213},{6,54},{7,215},{8,56}... | collective-permute-start | bytes 786440 | tf_op jit(solution)/shard_map/ppermute | solution.py:132
  42.2 0.0 collective-permute-done.2.refs_2_
  42.3 1.9 %collective-permute-start.3 = (f32[2,32,8,128]{3,2,1,0:T(8,128)S(1)}, f32[2,32,8,128]{3,2,1,0:T(8,128)S(1)}, u32[]{:S(2)}, u32[]{:S(2)}) collective-permute-start(f32[2,32,8,128]{3,2,1,0:T(8,128)S(1)} %collective-permute-done.2.refs_2_), channel_id=1, source_target_pairs={{0,208},{1,49},{2,210},{3,51},{4,212},{5,53},{6,214},{7,55},{8,216... | collective-permute-start | bytes 786440 | tf_op jit(solution)/shard_map/ppermute | solution.py:132
  44.2 4.2 %collective-permute-start.7 = (f32[3,2,17,8,128]{4,3,2,1,0:T(8,128)S(1)}, f32[3,2,17,8,128]{4,3,2,1,0:T(8,128)S(1)}, u32[]{:S(2)}, u32[]{:S(2)}) collective-permute-start(f32[3,2,17,8,128]{4,3,2,1,0:T(8,128)S(1)} %pad_maximum_fusion), channel_id=1, source_target_pairs={{0,16},{1,241},{2,18},{3,243},{4,20},{5,245},{6,22},{7,247},{8,24}... | collective-permute-start | bytes 1253384 | tf_op jit(solution)/shard_map/ppermute | solution.py:132
  48.5 1.9 %collective-permute-start.8 = (f32[3,2,17,8,128]{4,3,2,1,0:T(8,128)S(1)}, f32[3,2,17,8,128]{4,3,2,1,0:T(8,128)S(1)}, u32[]{:S(2)}, u32[]{:S(2)}) collective-permute-start(f32[3,2,17,8,128]{4,3,2,1,0:T(8,128)S(1)} %pad_maximum_fusion.1), channel_id=1, source_target_pairs={{0,240},{1,17},{2,242},{3,19},{4,244},{5,21},{6,246},{7,23},{8,248... | collective-permute-start | bytes 1253384 | tf_op jit(solution)/shard_map/ppermute | solution.py:132
  50.4 4.3 %collective-permute-done.1.refs_3_ = f32[2,32,8,128]{3,2,1,0:T(8,128)S(1)} collective-permute-done((f32[2,32,8,128]{3,2,1,0:T(8,128)S(1)}, f32[2,32,8,128]{3,2,1,0:T(8,128)S(1)}, u32[]{:S(2)}, u32[]{:S(2)}) %collective-permute-start.1) | collective-permute-done | bytes 262176 | tf_op jit(solution)/shard_map/ppermute | solution.py:132
  54.7 5.3 %collective-permute-done.3.refs_4_ = f32[2,32,8,128]{3,2,1,0:T(8,128)S(1)} collective-permute-done((f32[2,32,8,128]{3,2,1,0:T(8,128)S(1)}, f32[2,32,8,128]{3,2,1,0:T(8,128)S(1)}, u32[]{:S(2)}, u32[]{:S(2)}) %collective-permute-start.3) | collective-permute-done | bytes 262176 | tf_op jit(solution)/shard_map/ppermute | solution.py:132
  60.1 0.7 pad_maximum_fusion.3
  60.8 1.9 %collective-permute-start.5 = (f32[2,2,17,8,128]{4,3,2,1,0:T(8,128)}, f32[2,2,17,8,128]{4,3,2,1,0:T(8,128)S(1)}, u32[]{:S(2)}, u32[]{:S(2)}) collective-permute-start(f32[2,2,17,8,128]{4,3,2,1,0:T(8,128)} %pad_maximum_fusion.3), channel_id=1, source_target_pairs={{0,240},{1,17},{2,242},{3,19},{4,244},{5,21},{6,246},{7,23},{8,248... | collective-permute-start | bytes 835592 | tf_op jit(solution)/shard_map/ppermute | solution.py:132
  62.8 0.7 pad_maximum_fusion.2
  63.5 4.6 %collective-permute-start.4 = (f32[2,2,17,8,128]{4,3,2,1,0:T(8,128)}, f32[2,2,17,8,128]{4,3,2,1,0:T(8,128)S(1)}, u32[]{:S(2)}, u32[]{:S(2)}) collective-permute-start(f32[2,2,17,8,128]{4,3,2,1,0:T(8,128)} %pad_maximum_fusion.2), channel_id=1, source_target_pairs={{0,16},{1,241},{2,18},{3,243},{4,20},{5,245},{6,22},{7,247},{8,24}... | collective-permute-start | bytes 835592 | tf_op jit(solution)/shard_map/ppermute | solution.py:132
  68.0 2.0 %convert_reduce_fusion.1 = (s32[]{:T(128)}, s32[]{:T(128)}) fusion(s32[4096]{0:T(1024)} %param.7, s32[]{:T(128)S(6)} %add.104, s32[]{:T(128)} %bitcast.3), kind=kLoop, calls=%fused_computation.16 | loop fusion | flops 24574 | bytes 16400 | tf_op jit(solution)/shard_map/reduce_sum | solution.py:143
  73.8 1.3 %fusion = s32[]{:T(128)} fusion(s32[16,1024]{1,0:T(8,128)S(1)} %reshape.14, s32[]{:T(128)S(6)} %select_n.82, s32[]{:T(128)} %bitcast.3), kind=kLoop, calls=%fused_computation.19 | loop fusion | flops 3071 | bytes 4108 | tf_op jit(solution)/shard_map/reduce_sum | solution.py:144
  75.1 1.3 %stack.77.scal = s32[9]{0:T(128)S(1)} concatenate(s32[1]{0:T(128)} %get-tuple-element.31, s32[1]{0:T(128)} %bitcast.2, s32[1]{0:T(128)} %bitcast.4, s32[1]{0:T(128)} %bitcast.6, s32[1]{0:T(128)} %bitcast.7, s32[1]{0:T(128)} %bitcast.8, s32[1]{0:T(128)} %bitcast.9, s32[1]{0:T(128)} %bitcast.10, s32[1]{0:T(128)} %bitcast.11), dimensions={0} | concatenate | bytes 72 | tf_op jit(solution)/shard_map/stack | solution.py:145
  76.5 6.3 %collective-permute-start.6 = (f32[1,2,17,8,128]{4,3,2,1,0:T(8,128)S(1)}, f32[1,2,17,8,128]{4,3,2,1,0:T(8,128)S(1)}, u32[]{:S(2)}, u32[]{:S(2)}) collective-permute-start(f32[1,2,17,8,128]{4,3,2,1,0:T(8,128)S(1)} %get-tuple-element.21), channel_id=1, source_target_pairs={{0,32},{1,225},{2,34},{3,227},{4,36},{5,229},{6,38},{7,231},{8,40}... | collective-permute-start | bytes 417800 | tf_op jit(solution)/shard_map/ppermute | solution.py:132
  82.8 0.0 collective-permute-done.7.refs_5_
  82.8 0.0 collective-permute-done.8.refs_6_
  82.8 0.0 copy-start
  82.8 3.4 %copy-done = f32[1024,2048]{1,0:T(8,128)S(1)} copy-done((f32[1024,2048]{1,0:T(8,128)S(1)}, f32[1024,2048]{1,0:T(8,128)}, u32[]{:S(2)}) %copy-start) | copy-done | bytes 8388632
  86.2 0.0 copy-start.2
  86.2 0.9 copy-done.2
  87.2 0.0 copy-start.1
  87.2 8.1 %shard_map.46 = (f32[8,16,1024]{2,1,0:T(8,128)S(1)}, f32[8,16,1024]{2,1,0:T(8,128)S(1)}) custom-call(s32[9]{0:T(128)S(1)} %stack.77.scal, f32[2,32,8,128]{3,2,1,0:T(8,128)S(1)} %bitcast.47, f32[2,32,8,128]{3,2,1,0:T(8,128)S(1)} %collective-permute-done.refs_1_, f32[2,32,8,128]{3,2,1,0:T(8,128)S(1)} %collective-permute-done.2.refs_2_, ...), custom_call_target="tpu_custom_call" | custom-call | flops 2214592512 | bytes 8388608 | tf_op jit(solution)/shard_map/pallas_call | solution.py:89
  95.2 0.0 collective-permute-done.6.refs_2_
  95.2 0.0 collective-permute-done.5.refs_1_
  95.2 0.0 collective-permute-done.4.refs_0_
  95.3 0.0 copy-done.1
  95.3 7.2 %shard_map.47 = (f32[8,16,1024]{2,1,0:T(8,128)S(1)}, f32[8,16,1024]{2,1,0:T(8,128)S(1)}) custom-call(s32[9]{0:T(128)S(1)} %stack.77.scal, f32[2,2,17,8,128]{4,3,2,1,0:T(8,128)S(1)} %collective-permute-done.4.refs_0_, f32[2,2,17,8,128]{4,3,2,1,0:T(8,128)S(1)} %collective-permute-done.5.refs_1_, f32[1,2,17,8,128]{4,3,2,1,0:T(8,128)S(1)} %collective-permute-done.6.refs_2_, ...), custom_call_target="tpu_custom_call" | custom-call | flops 1006632960 | bytes 8388608 | tf_op jit(solution)/shard_map/pallas_call | solution.py:89
  102.5 1.9 %collective-permute-start.9 = (f32[8,16,1024]{2,1,0:T(8,128)S(1)}, f32[8,16,1024]{2,1,0:T(8,128)S(1)}, u32[]{:S(2)}, u32[]{:S(2)}) collective-permute-start(f32[8,16,1024]{2,1,0:T(8,128)S(1)} %get-tuple-element.12), channel_id=1, source_target_pairs={{0,1},{1,0},{2,3},{3,2},{4,5},{5,4},{6,7},{7,6},{8,9},{9,8},{10,11... | collective-permute-start | bytes 1572872 | tf_op jit(solution)/shard_map/ppermute | solution.py:109
  104.4 1.9 %collective-permute-done.9 = f32[8,16,1024]{2,1,0:T(8,128)S(1)} collective-permute-done((f32[8,16,1024]{2,1,0:T(8,128)S(1)}, f32[8,16,1024]{2,1,0:T(8,128)S(1)}, u32[]{:S(2)}, u32[]{:S(2)}) %collective-permute-start.9) | collective-permute-done | bytes 524320 | tf_op jit(solution)/shard_map/ppermute | solution.py:109
  106.3 0.1 add.121
  106.4 25.3 %all_to_all.5 = f32[8,16,1024]{2,1,0:T(8,128)S(1)} all-to-all(f32[8,16,1024]{2,1,0:T(8,128)S(1)} %add.121), channel_id=1, replica_groups={{0,2,4,6,8,10,12,14},{1,3,5,7,9,11,13,15},{16,18,20,22,24,26,28,30},{17..., dimensions={0} | all-to-all | bytes 1048576 | tf_op jit(solution)/shard_map/all_to_all | solution.py:111
  131.7 0.7 reduce_sum.49
  (7 shorter events, 0.2 us)
Async XLA Ops:
  0.0 35.0 %collective-permute-start = (f32[2,32,8,128]{3,2,1,0:T(8,128)}, f32[2,32,8,128]{3,2,1,0:T(8,128)S(1)}, u32[]{:S(2)}, u32[]{:S(2)}) collective-permute-start(f32[2,32,8,128]{3,2,1,0:T(8,128)} %bitcast.44), channel_id=1, source_target_pairs={{0,48},{1,209},{2,50},{3,211},{4,52},{5,213},{6,54},{7,215},{8,56}... | collective-permute-start | bytes 786440 | tf_op jit(solution)/shard_map/ppermute | solution.py:132
  18.8 23.5 %collective-permute-start.2 = (f32[2,32,8,128]{3,2,1,0:T(8,128)}, f32[2,32,8,128]{3,2,1,0:T(8,128)S(1)}, u32[]{:S(2)}, u32[]{:S(2)}) collective-permute-start(f32[2,32,8,128]{3,2,1,0:T(8,128)} %bitcast.45), channel_id=1, source_target_pairs={{0,208},{1,49},{2,210},{3,51},{4,212},{5,53},{6,214},{7,55},{8,216... | collective-permute-start | bytes 786440 | tf_op jit(solution)/shard_map/ppermute | solution.py:132
  35.0 19.7 %collective-permute-start.1 = (f32[2,32,8,128]{3,2,1,0:T(8,128)S(1)}, f32[2,32,8,128]{3,2,1,0:T(8,128)S(1)}, u32[]{:S(2)}, u32[]{:S(2)}) collective-permute-start(f32[2,32,8,128]{3,2,1,0:T(8,128)S(1)} %collective-permute-done.refs_1_), channel_id=1, source_target_pairs={{0,48},{1,209},{2,50},{3,211},{4,52},{5,213},{6,54},{7,215},{8,56}... | collective-permute-start | bytes 786440 | tf_op jit(solution)/shard_map/ppermute | solution.py:132
  42.3 17.8 %collective-permute-start.3 = (f32[2,32,8,128]{3,2,1,0:T(8,128)S(1)}, f32[2,32,8,128]{3,2,1,0:T(8,128)S(1)}, u32[]{:S(2)}, u32[]{:S(2)}) collective-permute-start(f32[2,32,8,128]{3,2,1,0:T(8,128)S(1)} %collective-permute-done.2.refs_2_), channel_id=1, source_target_pairs={{0,208},{1,49},{2,210},{3,51},{4,212},{5,53},{6,214},{7,55},{8,216... | collective-permute-start | bytes 786440 | tf_op jit(solution)/shard_map/ppermute | solution.py:132
  44.2 38.6 %collective-permute-start.7 = (f32[3,2,17,8,128]{4,3,2,1,0:T(8,128)S(1)}, f32[3,2,17,8,128]{4,3,2,1,0:T(8,128)S(1)}, u32[]{:S(2)}, u32[]{:S(2)}) collective-permute-start(f32[3,2,17,8,128]{4,3,2,1,0:T(8,128)S(1)} %pad_maximum_fusion), channel_id=1, source_target_pairs={{0,16},{1,241},{2,18},{3,243},{4,20},{5,245},{6,22},{7,247},{8,24}... | collective-permute-start | bytes 1253384 | tf_op jit(solution)/shard_map/ppermute | solution.py:132
  48.5 34.3 %collective-permute-start.8 = (f32[3,2,17,8,128]{4,3,2,1,0:T(8,128)S(1)}, f32[3,2,17,8,128]{4,3,2,1,0:T(8,128)S(1)}, u32[]{:S(2)}, u32[]{:S(2)}) collective-permute-start(f32[3,2,17,8,128]{4,3,2,1,0:T(8,128)S(1)} %pad_maximum_fusion.1), channel_id=1, source_target_pairs={{0,240},{1,17},{2,242},{3,19},{4,244},{5,21},{6,246},{7,23},{8,248... | collective-permute-start | bytes 1253384 | tf_op jit(solution)/shard_map/ppermute | solution.py:132
  60.8 34.4 %collective-permute-start.5 = (f32[2,2,17,8,128]{4,3,2,1,0:T(8,128)}, f32[2,2,17,8,128]{4,3,2,1,0:T(8,128)S(1)}, u32[]{:S(2)}, u32[]{:S(2)}) collective-permute-start(f32[2,2,17,8,128]{4,3,2,1,0:T(8,128)} %pad_maximum_fusion.3), channel_id=1, source_target_pairs={{0,240},{1,17},{2,242},{3,19},{4,244},{5,21},{6,246},{7,23},{8,248... | collective-permute-start | bytes 835592 | tf_op jit(solution)/shard_map/ppermute | solution.py:132
  63.5 31.8 %collective-permute-start.4 = (f32[2,2,17,8,128]{4,3,2,1,0:T(8,128)}, f32[2,2,17,8,128]{4,3,2,1,0:T(8,128)S(1)}, u32[]{:S(2)}, u32[]{:S(2)}) collective-permute-start(f32[2,2,17,8,128]{4,3,2,1,0:T(8,128)} %pad_maximum_fusion.2), channel_id=1, source_target_pairs={{0,16},{1,241},{2,18},{3,243},{4,20},{5,245},{6,22},{7,247},{8,24}... | collective-permute-start | bytes 835592 | tf_op jit(solution)/shard_map/ppermute | solution.py:132
  76.5 18.8 %collective-permute-start.6 = (f32[1,2,17,8,128]{4,3,2,1,0:T(8,128)S(1)}, f32[1,2,17,8,128]{4,3,2,1,0:T(8,128)S(1)}, u32[]{:S(2)}, u32[]{:S(2)}) collective-permute-start(f32[1,2,17,8,128]{4,3,2,1,0:T(8,128)S(1)} %get-tuple-element.21), channel_id=1, source_target_pairs={{0,32},{1,225},{2,34},{3,227},{4,36},{5,229},{6,38},{7,231},{8,40}... | collective-permute-start | bytes 417800 | tf_op jit(solution)/shard_map/ppermute | solution.py:132
  82.8 3.4 %copy-start = (f32[1024,2048]{1,0:T(8,128)S(1)}, f32[1024,2048]{1,0:T(8,128)}, u32[]{:S(2)}) copy-start(f32[1024,2048]{1,0:T(8,128)} %refs_3_.1) | copy-start | bytes 25165828
  86.2 0.9 copy-start.2
  87.2 8.1 %copy-start.1 = (f32[1024,2048]{1,0:T(8,128)S(1)}, f32[1024,2048]{1,0:T(8,128)}, u32[]{:S(2)}) copy-start(f32[1024,2048]{1,0:T(8,128)} %refs_3_.1) | copy-start | bytes 25165828
  102.5 3.8 %collective-permute-start.9 = (f32[8,16,1024]{2,1,0:T(8,128)S(1)}, f32[8,16,1024]{2,1,0:T(8,128)S(1)}, u32[]{:S(2)}, u32[]{:S(2)}) collective-permute-start(f32[8,16,1024]{2,1,0:T(8,128)S(1)} %get-tuple-element.12), channel_id=1, source_target_pairs={{0,1},{1,0},{2,3},{3,2},{4,5},{5,4},{6,7},{7,6},{8,9},{9,8},{10,11... | collective-permute-start | bytes 1572872 | tf_op jit(solution)/shard_map/ppermute | solution.py:109

commit v3 on v2

v3 whole, which is shorter than its diff:
```python
import functools

import jax
import jax.numpy as jnp
from jax import lax
from jax.experimental import pallas as pl
from jax.experimental.pallas import tpu as pltpu
from jax.sharding import PartitionSpec as P

LANES = 128
AB_TILE = 256
IRREPS = 8
OFF, N_LOW, COL0, COL1, COL2, TILE = 0, 1, 2, 3, 4, 5


def position():
    z = lax.axis_index("vp")
    core = lax.axis_index("cd") & 1
    return z, core, 1 - 2 * core


def prepare_kernel(owners, win_tiles, ab_ref, cd_ref, w_ref, scal, hi, lo, below):
    step = pl.program_id(0)
    width = w_ref.shape[1]
    n_cd_tiles = cd_ref.shape[0]
    per_owner = ab_ref.shape[0] // owners

    @pl.when(step == 0)
    def count():
        z, core, d = position()

        def total(mask):
            return jnp.sum(jnp.where(mask, 1.0, 0.0)).astype(jnp.int32)

        labels = cd_ref[...]
        below[0] = jnp.int32(0)
        below[IRREPS] = jnp.int32(n_cd_tiles * LANES)
        for r in range(1, IRREPS):
            below[r] = total(labels < r)

        def low_of(v):
            rows = ab_ref[pl.ds(pl.multiple_of(v * per_owner, per_owner), per_owner)]
            return jnp.min(rows.astype(jnp.float32)).astype(jnp.int32), rows

        def start_of(low):
            start = jnp.minimum(below[low], n_cd_tiles * LANES - width)
            return start, jnp.minimum(start // LANES, n_cd_tiles - win_tiles)

        low, rows = low_of(z)
        start, tile = start_of(low)
        scal[OFF] = start - tile * LANES
        scal[N_LOW] = total(rows == low)
        scal[COL0] = below[low] - start
        scal[COL1] = below[low + 1] - start
        scal[COL2] = below[low + 2] - start
        scal[TILE] = tile
        for i, k in enumerate((1, -1, 2)):
            scal[TILE + 1 + i] = start_of(low_of((z + k * d + 2 * owners) % owners)[0])[1]

    rows = lax.broadcasted_iota(jnp.int32, (AB_TILE, 1), 0) + step * AB_TILE
    first = jnp.where(rows < scal[N_LOW], scal[COL0], scal[COL1])
    last = jnp.where(rows < scal[N_LOW], scal[COL1], scal[COL2])
    for at in range(0, width, LANES):
        cols = lax.broadcasted_iota(jnp.int32, (AB_TILE, LANES), 1) + at
        w = jnp.where((cols >= first) & (cols < last), w_ref[:, at : at + LANES], 0.0)
        high = w.astype(jnp.bfloat16)
        hi[:, at : at + LANES] = high
        lo[:, at : at + LANES] = (w - high.astype(jnp.float32)).astype(jnp.bfloat16)


def prepare(irrep_ab, irrep_cd, w_slab, owners):
    ab, width = w_slab.shape
    labels_ab = irrep_ab.reshape(-1, LANES)
    labels_cd = irrep_cd.reshape(-1, LANES)
    tile_spec = pl.BlockSpec((AB_TILE, width), lambda i: (i, 0))
    half = jax.ShapeDtypeStruct((ab, width), jnp.bfloat16)
    return pl.pallas_call(
        functools.partial(prepare_kernel, owners, width // LANES + 1),
        grid=(ab // AB_TILE,),
        in_specs=[
            pl.BlockSpec(labels_ab.shape, lambda i: (0, 0)),
            pl.BlockSpec(labels_cd.shape, lambda i: (0, 0)),
            tile_spec,
        ],
        out_specs=[pl.BlockSpec(memory_space=pltpu.SMEM), tile_spec, tile_spec],
        out_shape=[jax.ShapeDtypeStruct((16,), jnp.int32), half, half],
        scratch_shapes=[pltpu.SMEM((16,), jnp.int32)],
        compiler_params=pltpu.CompilerParams(vmem_limit_bytes=24 * 1024 * 1024),
        cost_estimate=pl.CostEstimate(flops=8 * ab * width, bytes_accessed=8 * ab * width, transcendentals=0),
    )(labels_ab, labels_cd, w_slab)


def cut_kernel(picks, n_src, scal, *refs):
    srcs, outs = refs[:n_src], refs[n_src:]
    for out, (place, chosen) in zip(outs, picks):
        at = scal[TILE + place]
        for i, s in enumerate(chosen):
            out[i] = srcs[s][:, pl.ds(at, out.shape[2])]


def cut(scal, sources, picks, win_tiles):
    groups, _, _, _ = sources[0].shape
    outs = [jax.ShapeDtypeStruct((len(p[1]), groups, win_tiles, 8, LANES), jnp.float32) for p in picks]
    vmem = pl.BlockSpec(memory_space=pltpu.VMEM)
    size = sum(4 * o.size for o in outs)
    return pl.pallas_call(
        functools.partial(cut_kernel, picks, len(sources)),
        in_specs=[pl.BlockSpec(memory_space=pltpu.SMEM)] + [vmem] * len(sources),
        out_specs=[vmem] * len(outs),
        out_shape=outs,
        compiler_params=pltpu.CompilerParams(vmem_limit_bytes=8 * 1024 * 1024),
        cost_estimate=pl.CostEstimate(flops=0, bytes_accessed=2 * size, transcendentals=0),
    )(scal, *sources)


def contract_kernel(rels, shapes, carried, scal, *refs):
    n_src = len(shapes)
    srcs, refs = refs[:n_src], refs[n_src:]
    w_hi, w_lo, refs = refs[0], refs[1], refs[2:]
    if carried:
        old_mine, old_other, refs = refs[0], refs[1], refs[2:]
    mine, other, amps = refs
    width = w_hi.shape[1]
    padded = amps.shape[1] // 2
    tiles = width // LANES
    share = mine.shape[1]

    @pl.when(pl.program_id(0) == 0)
    def build():
        off, tile0 = scal[OFF], scal[TILE]
        lane = lax.broadcasted_iota(jnp.int32, (padded, LANES), 1)
        keep = lane < LANES - off
        turn = lax.rem(LANES - off, LANES)
        rolled = None
        for j in range(tiles + 1):
            pieces = []
            for ref, count in zip(srcs, shapes):
                if count is None:
                    pieces.append(ref[:, pl.ds(tile0 + j, 1)].reshape(share, LANES))
                else:
                    pieces += [ref[i, :, j].reshape(share, LANES) for i in range(count)]
            if padded > share * len(rels):
                pieces.append(jnp.zeros((padded - share * len(rels), LANES), jnp.float32))
            new = pltpu.roll(jnp.concatenate(pieces, axis=0), turn, 1)
            if rolled is not None:
                value = jnp.where(keep, rolled, new).T
                high = value.astype(jnp.bfloat16)
                rows = slice((j - 1) * LANES, j * LANES)
                amps[rows, :padded] = high
                amps[rows, padded:] = (value - high.astype(jnp.float32)).astype(jnp.bfloat16)
            rolled = new

    dot = functools.partial(jnp.dot, preferred_element_type=jnp.float32)
    both = dot(w_hi[...], amps[...])
    turned = both[:, :padded] + both[:, padded:] + dot(w_lo[...], amps[:, :padded])
    out = turned.T
    if carried:
        mine[...] = old_mine[...]
        other[...] = old_other[...]
    z, core, d = position()
    for i, rel in enumerate(rels):
        block = (z + rel * d + 32) & 15
        value = out[i * share : (i + 1) * share]

        @pl.when((block & 1) == core)
        def keep_block():
            mine[pl.ds(block >> 1, 1)] = value[None]

        @pl.when((block & 1) != core)
        def send_block():
            other[pl.ds(block >> 1, 1)] = value[None]


def contract(scal, sources, rels, w_hi, w_lo, old=()):
    ab, width = w_hi.shape
    shapes = [None if s.ndim == 4 else s.shape[0] for s in sources]
    share = 16
    rows = share * len(rels)
    padded = -(-rows // LANES) * LANES
    whole = [pl.BlockSpec(s.shape, functools.partial(lambda n, i: (0,) * n, s.ndim)) for s in sources]
    tile_spec = pl.BlockSpec((AB_TILE, width), lambda i: (i, 0))
    out_spec = pl.BlockSpec((8, share, AB_TILE), lambda i: (0, 0, i))
    out_shape = jax.ShapeDtypeStruct((8, share, ab), jnp.float32)
    return pl.pallas_call(
        functools.partial(contract_kernel, rels, shapes, bool(old)),
        grid=(ab // AB_TILE,),
        in_specs=[pl.BlockSpec(memory_space=pltpu.SMEM)] + whole + [tile_spec] * 2 + [out_spec] * len(old),
        out_specs=[out_spec, out_spec],
        out_shape=[out_shape, out_shape],
        scratch_shapes=[pltpu.VMEM((width, 2 * padded), jnp.bfloat16)],
        compiler_params=pltpu.CompilerParams(vmem_limit_bytes=24 * 1024 * 1024),
        cost_estimate=pl.CostEstimate(
            flops=6 * rows * width * ab, bytes_accessed=4 * ab * width, transcendentals=0
        ),
    )(scal, *sources, w_hi, w_lo, *old)


def reduce_rows(mine, other):
    n_cd = lax.axis_size("cd")
    pair = [(i, i ^ 1) for i in range(n_cd)]
    both = mine + lax.ppermute(other, "cd", pair)
    groups = [[c for c in range(n_cd) if c % 2 == p] for p in range(2)]
    parts = lax.all_to_all(both, "cd", 0, 0, axis_index_groups=groups)
    return jnp.sum(parts, axis=0)


def per_device(t2_amps, w_slab, irrep_ab, irrep_cd):
    n_vp = lax.axis_size("vp")
    n_cd = lax.axis_size("cd")
    rows_dev, cd_dev = t2_amps.shape
    win_tiles = w_slab.shape[1] // LANES + 1

    def move(array, k):
        pairs = [
            (v * n_cd + e, ((v + (k if e % 2 == 0 else -k)) % n_vp) * n_cd + e)
            for v in range(n_vp)
            for e in range(n_cd)
        ]
        return lax.ppermute(array, ("vp", "cd"), pairs)

    own = t2_amps.reshape(rows_dev // 8, 8, cd_dev // LANES, LANES).transpose(0, 2, 1, 3)
    x1 = move(own, 3)
    y1 = move(own, -3)
    scal, w_hi, w_lo = prepare(irrep_ab, irrep_cd, w_slab, n_vp)
    x2 = move(x1, 3)
    y2 = move(y1, -3)
    to_x, to_y = cut(scal, [own, x1, y1], [(1, (0, 1, 2)), (2, (0, 1, 2))], win_tiles)
    near_x = move(to_x, 1)
    near_y = move(to_y, -1)
    to_x, to_y, to_edge = cut(scal, [x2, y2], [(1, (0, 1)), (2, (0, 1)), (3, (0,))], win_tiles)
    far_x = move(to_x, 1)
    far_y = move(to_y, -1)
    edge = move(to_edge, 2)
    first = contract(
        scal,
        [own, x1, y1, x2, y2, near_x, near_y],
        [0, -3, 3, -6, 6, -1, -4, 2, 1, -2, 4],
        w_hi,
        w_lo,
    )
    mine, other = contract(scal, [far_x, far_y, edge], [-7, 5, -5, 7, -8], w_hi, w_lo, first)
    return reduce_rows(mine, other)


def solution(mesh):
    placed = (P(("op", "vp"), "cd"), P("vp", "cd"), P(), P("cd"))
    return jax.shard_map(
        per_device, mesh=mesh, in_specs=placed, out_specs=P(("op", "cd"), "vp"), check_vma=False
    )
```

time: 133 us -> 122 us (0.917)
  waiting for transfers between devices: 12.9 us -> 26.5 us
  between operations: 11.5 us -> 0.17 us
  other arithmetic: 6.52 us -> 0.73 us
  local copies, waits for them, and re-layouts: 10.2 us -> 4.93 us
    ppermute x9, waiting for transfers between devices: 11.1 us -> 25 us  [move(): return lax.ppermute(array, ('vp', 'cd'), pairs)]
    reduce_sum x3 -> x0, other arithmetic: 4.26 us -> none  [the longest x1 2 us: per_device(): below2 = jnp.sum((irrep_cd <= low + 1).astype(jnp.int32))]
    another operation x5 -> x0, local copies, waits for them, and re-layouts: 2.43 us -> none  [the longest x1 1.33 us: per_device(): jnp.stack([tile0, start - tile0 * LANES, n_low, counts[z] - start, below1...]
    dynamic_slice x4 -> x0, local copies, waits for them, and re-layouts: 2.42 us -> none  [the longest x1 0.69 us: window(): at = tile_of[(z + k * d + 2 * n_vp) % n_vp]]
    another operation x4 -> x0, other arithmetic: 1.52 us -> none  [the longest x1 0.74 us: per_device(): far_y = move(jnp.stack([window(b, -1) for b in (x2, y2)]), -1)]
    ppermute x9, starting transfers between devices: 48.7 us -> 47.2 us  [move(): return lax.ppermute(array, ('vp', 'cd'), pairs)]
    unnamed x6 -> x8, local copies, waits for them, and re-layouts: 4.33 us -> 4.93 us
    pallas_call x2 -> x5, Pallas kernels: 15.3 us -> 15.7 us  [the longest x2 11.2 us: contract(): pl.pallas_call(functools.partial(contract_kernel, rels, shapes, bool(old)...]
  transfers between devices with their start and end apart: 10 -> 10, of which waited for: 4 -> 5; matrix products, arithmetic and copies ran while one was open for 9% -> 0% of each run, Pallas kernels for 6% -> 9%
where the time goes in v3:
time: 122 us
  starting transfers between devices  49.8 us (41%)
  waiting for transfers between devices  26.5 us (22%)
  blocking collectives  24.1 us (20%)
  Pallas kernels  15.7 us (13%)
  local copies, waits for them, and re-layouts  4.93 us (4%)
    ppermute x9, starting transfers between devices, move(): return lax.ppermute(array, ('vp', 'cd'), pairs)  47.2 us
    ppermute x9, waiting for transfers between devices, move(): return lax.ppermute(array, ('vp', 'cd'), pairs)  25 us
    all_to_all x1, blocking collectives, reduce_rows(): parts = lax.all_to_all(both, 'cd', 0, 0, axis_index_groups=groups)  24.1 us
    pallas_call x2, Pallas kernels, contract(): pl.pallas_call(functools.partial(contract_kernel, rels, shapes, bool(old)...  11.2 us
    unnamed x8, local copies, waits for them, and re-layouts  4.93 us
    pallas_call x1, Pallas kernels, prepare(): pl.pallas_call(functools.partial(prepare_kernel, owners, width // LANES +...  3.33 us
    ppermute x1, starting transfers between devices, reduce_rows(): both = mine + lax.ppermute(other, 'cd', pair)  2.59 us
  transfers between devices with their start and end apart: 10, of which 5 were waited for; matrix products, arithmetic and copies ran while one was open for 0% of the time, Pallas kernels for 9%

profile of v3, /device:TPU:1, one launch (start us, length us, event | category | flops | bytes accessed | tf_op | source)
XLA Modules:
  0.0 121.9 jit_solution(5710534177583189881)
XLA Ops:
  0.0 18.7 %collective-permute-start = (f32[2,32,8,128]{3,2,1,0:T(8,128)}, f32[2,32,8,128]{3,2,1,0:T(8,128)S(1)}, u32[]{:S(2)}, u32[]{:S(2)}) collective-permute-start(f32[2,32,8,128]{3,2,1,0:T(8,128)} %bitcast.5), channel_id=1, source_target_pairs={{0,48},{1,209},{2,50},{3,211},{4,52},{5,213},{6,54},{7,215},{8,56}... | collective-permute-start | bytes 786440 | tf_op jit(solution)/shard_map/ppermute | solution.py:219
  18.7 1.9 %collective-permute-start.2 = (f32[2,32,8,128]{3,2,1,0:T(8,128)}, f32[2,32,8,128]{3,2,1,0:T(8,128)S(1)}, u32[]{:S(2)}, u32[]{:S(2)}) collective-permute-start(f32[2,32,8,128]{3,2,1,0:T(8,128)} %bitcast.6), channel_id=1, source_target_pairs={{0,208},{1,49},{2,210},{3,51},{4,212},{5,53},{6,214},{7,55},{8,216... | collective-permute-start | bytes 786440 | tf_op jit(solution)/shard_map/ppermute | solution.py:219
  20.7 0.0 copy-start
  20.7 3.4 %copy-done = f32[1024,2048]{1,0:T(8,128)S(1)} copy-done((f32[1024,2048]{1,0:T(8,128)S(1)}, f32[1024,2048]{1,0:T(8,128)}, u32[]{:S(2)}) %copy-start) | copy-done | bytes 8388632
  24.1 0.0 copy-start.2
  24.1 0.8 copy-done.2
  24.9 0.0 copy-start.3
  24.9 0.7 copy-done.3
  25.6 0.0 copy-start.1
  25.6 3.3 %shard_map.46 = (s32[16]{0:T(128)S(1)}, bf16[1024,2048]{1,0:T(8,128)(2,1)S(1)}, bf16[1024,2048]{1,0:T(8,128)(2,1)S(1)}) custom-call(s32[128,128]{1,0:T(8,128)S(1)} %bitcast.9, s32[32,128]{1,0:T(8,128)S(1)} %bitcast.10, f32[1024,2048]{1,0:T(8,128)S(1)} %copy-done), custom_call_target="tpu_custom_call" | custom-call | flops 16777216 | bytes 16777216 | tf_op jit(solution)/shard_map/pallas_call | solution.py:77
  29.0 6.1 %collective-permute-done.refs_1_ = f32[2,32,8,128]{3,2,1,0:T(8,128)S(1)} collective-permute-done((f32[2,32,8,128]{3,2,1,0:T(8,128)}, f32[2,32,8,128]{3,2,1,0:T(8,128)S(1)}, u32[]{:S(2)}, u32[]{:S(2)}) %collective-permute-start) | collective-permute-done | bytes 262176 | tf_op jit(solution)/shard_map/ppermute | solution.py:219
  35.0 4.1 %collective-permute-done.2.refs_2_ = f32[2,32,8,128]{3,2,1,0:T(8,128)S(1)} collective-permute-done((f32[2,32,8,128]{3,2,1,0:T(8,128)}, f32[2,32,8,128]{3,2,1,0:T(8,128)S(1)}, u32[]{:S(2)}, u32[]{:S(2)}) %collective-permute-start.2) | collective-permute-done | bytes 262176 | tf_op jit(solution)/shard_map/ppermute | solution.py:219
  39.1 0.0 copy-done.1
  39.1 0.6 shard_map.48
  39.7 1.9 %collective-permute-start.7 = (f32[3,2,17,8,128]{4,3,2,1,0:T(8,128)S(1)}, f32[3,2,17,8,128]{4,3,2,1,0:T(8,128)S(1)}, u32[]{:S(2)}, u32[]{:S(2)}) collective-permute-start(f32[3,2,17,8,128]{4,3,2,1,0:T(8,128)S(1)} %get-tuple-element.23), channel_id=1, source_target_pairs={{0,16},{1,241},{2,18},{3,243},{4,20},{5,245},{6,22},{7,247},{8,24}... | collective-permute-start | bytes 1253384 | tf_op jit(solution)/shard_map/ppermute | solution.py:219
  41.7 3.4 %collective-permute-start.8 = (f32[3,2,17,8,128]{4,3,2,1,0:T(8,128)S(1)}, f32[3,2,17,8,128]{4,3,2,1,0:T(8,128)S(1)}, u32[]{:S(2)}, u32[]{:S(2)}) collective-permute-start(f32[3,2,17,8,128]{4,3,2,1,0:T(8,128)S(1)} %get-tuple-element.24), channel_id=1, source_target_pairs={{0,240},{1,17},{2,242},{3,19},{4,244},{5,21},{6,246},{7,23},{8,248... | collective-permute-start | bytes 1253384 | tf_op jit(solution)/shard_map/ppermute | solution.py:219
  45.0 5.4 %collective-permute-start.1 = (f32[2,32,8,128]{3,2,1,0:T(8,128)S(1)}, f32[2,32,8,128]{3,2,1,0:T(8,128)S(1)}, u32[]{:S(2)}, u32[]{:S(2)}) collective-permute-start(f32[2,32,8,128]{3,2,1,0:T(8,128)S(1)} %collective-permute-done.refs_1_), channel_id=1, source_target_pairs={{0,48},{1,209},{2,50},{3,211},{4,52},{5,213},{6,54},{7,215},{8,56}... | collective-permute-start | bytes 786440 | tf_op jit(solution)/shard_map/ppermute | solution.py:219
  50.4 1.9 %collective-permute-start.3 = (f32[2,32,8,128]{3,2,1,0:T(8,128)S(1)}, f32[2,32,8,128]{3,2,1,0:T(8,128)S(1)}, u32[]{:S(2)}, u32[]{:S(2)}) collective-permute-start(f32[2,32,8,128]{3,2,1,0:T(8,128)S(1)} %collective-permute-done.2.refs_2_), channel_id=1, source_target_pairs={{0,208},{1,49},{2,210},{3,51},{4,212},{5,53},{6,214},{7,55},{8,216... | collective-permute-start | bytes 786440 | tf_op jit(solution)/shard_map/ppermute | solution.py:219
  52.3 7.2 %collective-permute-done.1.refs_0_.refs_3_ = f32[2,32,8,128]{3,2,1,0:T(8,128)S(1)} collective-permute-done((f32[2,32,8,128]{3,2,1,0:T(8,128)S(1)}, f32[2,32,8,128]{3,2,1,0:T(8,128)S(1)}, u32[]{:S(2)}, u32[]{:S(2)}) %collective-permute-start.1) | collective-permute-done | bytes 262176 | tf_op jit(solution)/shard_map/ppermute | solution.py:219
  59.5 7.6 %collective-permute-done.3.refs_1_.refs_4_ = f32[2,32,8,128]{3,2,1,0:T(8,128)S(1)} collective-permute-done((f32[2,32,8,128]{3,2,1,0:T(8,128)S(1)}, f32[2,32,8,128]{3,2,1,0:T(8,128)S(1)}, u32[]{:S(2)}, u32[]{:S(2)}) %collective-permute-start.3) | collective-permute-done | bytes 262176 | tf_op jit(solution)/shard_map/ppermute | solution.py:219
  67.1 0.6 shard_map.47
  67.7 9.0 %collective-permute-start.4 = (f32[2,2,17,8,128]{4,3,2,1,0:T(8,128)S(1)}, f32[2,2,17,8,128]{4,3,2,1,0:T(8,128)S(1)}, u32[]{:S(2)}, u32[]{:S(2)}) collective-permute-start(f32[2,2,17,8,128]{4,3,2,1,0:T(8,128)S(1)} %get-tuple-element.18), channel_id=1, source_target_pairs={{0,16},{1,241},{2,18},{3,243},{4,20},{5,245},{6,22},{7,247},{8,24}... | collective-permute-start | bytes 835592 | tf_op jit(solution)/shard_map/ppermute | solution.py:219
  76.7 1.9 %collective-permute-start.5 = (f32[2,2,17,8,128]{4,3,2,1,0:T(8,128)S(1)}, f32[2,2,17,8,128]{4,3,2,1,0:T(8,128)S(1)}, u32[]{:S(2)}, u32[]{:S(2)}) collective-permute-start(f32[2,2,17,8,128]{4,3,2,1,0:T(8,128)S(1)} %get-tuple-element.19), channel_id=1, source_target_pairs={{0,240},{1,17},{2,242},{3,19},{4,244},{5,21},{6,246},{7,23},{8,248... | collective-permute-start | bytes 835592 | tf_op jit(solution)/shard_map/ppermute | solution.py:219
  78.6 3.1 %collective-permute-start.6 = (f32[1,2,17,8,128]{4,3,2,1,0:T(8,128)S(1)}, f32[1,2,17,8,128]{4,3,2,1,0:T(8,128)S(1)}, u32[]{:S(2)}, u32[]{:S(2)}) collective-permute-start(f32[1,2,17,8,128]{4,3,2,1,0:T(8,128)S(1)} %get-tuple-element.20), channel_id=1, source_target_pairs={{0,32},{1,225},{2,34},{3,227},{4,36},{5,229},{6,38},{7,231},{8,40}... | collective-permute-start | bytes 417800 | tf_op jit(solution)/shard_map/ppermute | solution.py:219
  81.7 0.0 collective-permute-done.7.refs_5_
  81.7 0.0 collective-permute-done.8.refs_6_
  81.7 6.6 %shard_map.49 = (f32[8,16,1024]{2,1,0:T(8,128)S(1)}, f32[8,16,1024]{2,1,0:T(8,128)S(1)}) custom-call(s32[16]{0:T(128)S(1)} %get-tuple-element.17.scal, f32[2,32,8,128]{3,2,1,0:T(8,128)S(1)} %bitcast.8, f32[2,32,8,128]{3,2,1,0:T(8,128)S(1)} %collective-permute-done.refs_1_, f32[2,32,8,128]{3,2,1,0:T(8,128)S(1)} %collective-permute-done.2.refs_2_, ...), custom_call_target="tpu_custom_call" | custom-call | flops 2214592512 | bytes 8388608 | tf_op jit(solution)/shard_map/pallas_call | solution.py:184
  88.3 0.0 collective-permute-done.6.refs_2_
  88.3 0.0 collective-permute-done.4.refs_0_
  88.3 0.0 collective-permute-done.5.refs_1_
  88.3 4.6 %shard_map.50 = (f32[8,16,1024]{2,1,0:T(8,128)S(1)}, f32[8,16,1024]{2,1,0:T(8,128)S(1)}) custom-call(s32[16]{0:T(128)S(1)} %get-tuple-element.17.scal, f32[2,2,17,8,128]{4,3,2,1,0:T(8,128)S(1)} %collective-permute-done.4.refs_0_, f32[2,2,17,8,128]{4,3,2,1,0:T(8,128)S(1)} %collective-permute-done.5.refs_1_, ...), custom_call_target="tpu_custom_call" | custom-call | flops 1006632960 | bytes 8388608 | tf_op jit(solution)/shard_map/pallas_call | solution.py:184
  92.9 2.6 %collective-permute-start.9 = (f32[8,16,1024]{2,1,0:T(8,128)S(1)}, f32[8,16,1024]{2,1,0:T(8,128)S(1)}, u32[]{:S(2)}, u32[]{:S(2)}) collective-permute-start(f32[8,16,1024]{2,1,0:T(8,128)S(1)} %get-tuple-element.28), channel_id=1, source_target_pairs={{0,1},{1,0},{2,3},{3,2},{4,5},{5,4},{6,7},{7,6},{8,9},{9,8},{10,11... | collective-permute-start | bytes 1572872 | tf_op jit(solution)/shard_map/ppermute | solution.py:201
  95.5 1.5 %collective-permute-done.9 = f32[8,16,1024]{2,1,0:T(8,128)S(1)} collective-permute-done((f32[8,16,1024]{2,1,0:T(8,128)S(1)}, f32[8,16,1024]{2,1,0:T(8,128)S(1)}, u32[]{:S(2)}, u32[]{:S(2)}) %collective-permute-start.9) | collective-permute-done | bytes 524320 | tf_op jit(solution)/shard_map/ppermute | solution.py:201
  97.0 0.1 add.3
  97.1 24.1 %all_to_all.5 = f32[8,16,1024]{2,1,0:T(8,128)S(1)} all-to-all(f32[8,16,1024]{2,1,0:T(8,128)S(1)} %add.3), channel_id=1, replica_groups={{0,2,4,6,8,10,12,14},{1,3,5,7,9,11,13,15},{16,18,20,22,24,26,28,30},{17..., dimensions={0} | all-to-all | bytes 1048576 | tf_op jit(solution)/shard_map/all_to_all | solution.py:203
  121.2 0.7 reduce_sum.9
Async XLA Ops:
  0.0 35.0 %collective-permute-start = (f32[2,32,8,128]{3,2,1,0:T(8,128)}, f32[2,32,8,128]{3,2,1,0:T(8,128)S(1)}, u32[]{:S(2)}, u32[]{:S(2)}) collective-permute-start(f32[2,32,8,128]{3,2,1,0:T(8,128)} %bitcast.5), channel_id=1, source_target_pairs={{0,48},{1,209},{2,50},{3,211},{4,52},{5,213},{6,54},{7,215},{8,56}... | collective-permute-start | bytes 786440 | tf_op jit(solution)/shard_map/ppermute | solution.py:219
  18.7 20.4 %collective-permute-start.2 = (f32[2,32,8,128]{3,2,1,0:T(8,128)}, f32[2,32,8,128]{3,2,1,0:T(8,128)S(1)}, u32[]{:S(2)}, u32[]{:S(2)}) collective-permute-start(f32[2,32,8,128]{3,2,1,0:T(8,128)} %bitcast.6), channel_id=1, source_target_pairs={{0,208},{1,49},{2,210},{3,51},{4,212},{5,53},{6,214},{7,55},{8,216... | collective-permute-start | bytes 786440 | tf_op jit(solution)/shard_map/ppermute | solution.py:219
  20.7 3.4 %copy-start = (f32[1024,2048]{1,0:T(8,128)S(1)}, f32[1024,2048]{1,0:T(8,128)}, u32[]{:S(2)}) copy-start(f32[1024,2048]{1,0:T(8,128)} %w_ref.1) | copy-start | bytes 25165828
  24.1 0.8 copy-start.2
  24.9 0.7 copy-start.3
  25.6 13.5 %copy-start.1 = (f32[16,4096]{1,0:T(8,128)S(1)}, f32[16,4096]{1,0:T(8,128)}, u32[]{:S(2)}) copy-start(f32[16,4096]{1,0:T(8,128)} %param.4) | copy-start | bytes 786436
  39.7 42.0 %collective-permute-start.7 = (f32[3,2,17,8,128]{4,3,2,1,0:T(8,128)S(1)}, f32[3,2,17,8,128]{4,3,2,1,0:T(8,128)S(1)}, u32[]{:S(2)}, u32[]{:S(2)}) collective-permute-start(f32[3,2,17,8,128]{4,3,2,1,0:T(8,128)S(1)} %get-tuple-element.23), channel_id=1, source_target_pairs={{0,16},{1,241},{2,18},{3,243},{4,20},{5,245},{6,22},{7,247},{8,24}... | collective-permute-start | bytes 1253384 | tf_op jit(solution)/shard_map/ppermute | solution.py:219
  41.7 40.0 %collective-permute-start.8 = (f32[3,2,17,8,128]{4,3,2,1,0:T(8,128)S(1)}, f32[3,2,17,8,128]{4,3,2,1,0:T(8,128)S(1)}, u32[]{:S(2)}, u32[]{:S(2)}) collective-permute-start(f32[3,2,17,8,128]{4,3,2,1,0:T(8,128)S(1)} %get-tuple-element.24), channel_id=1, source_target_pairs={{0,240},{1,17},{2,242},{3,19},{4,244},{5,21},{6,246},{7,23},{8,248... | collective-permute-start | bytes 1253384 | tf_op jit(solution)/shard_map/ppermute | solution.py:219
  45.0 14.5 %collective-permute-start.1 = (f32[2,32,8,128]{3,2,1,0:T(8,128)S(1)}, f32[2,32,8,128]{3,2,1,0:T(8,128)S(1)}, u32[]{:S(2)}, u32[]{:S(2)}) collective-permute-start(f32[2,32,8,128]{3,2,1,0:T(8,128)S(1)} %collective-permute-done.refs_1_), channel_id=1, source_target_pairs={{0,48},{1,209},{2,50},{3,211},{4,52},{5,213},{6,54},{7,215},{8,56}... | collective-permute-start | bytes 786440 | tf_op jit(solution)/shard_map/ppermute | solution.py:219
  50.4 16.7 %collective-permute-start.3 = (f32[2,32,8,128]{3,2,1,0:T(8,128)S(1)}, f32[2,32,8,128]{3,2,1,0:T(8,128)S(1)}, u32[]{:S(2)}, u32[]{:S(2)}) collective-permute-start(f32[2,32,8,128]{3,2,1,0:T(8,128)S(1)} %collective-permute-done.2.refs_2_), channel_id=1, source_target_pairs={{0,208},{1,49},{2,210},{3,51},{4,212},{5,53},{6,214},{7,55},{8,216... | collective-permute-start | bytes 786440 | tf_op jit(solution)/shard_map/ppermute | solution.py:219
  67.7 20.6 %collective-permute-start.4 = (f32[2,2,17,8,128]{4,3,2,1,0:T(8,128)S(1)}, f32[2,2,17,8,128]{4,3,2,1,0:T(8,128)S(1)}, u32[]{:S(2)}, u32[]{:S(2)}) collective-permute-start(f32[2,2,17,8,128]{4,3,2,1,0:T(8,128)S(1)} %get-tuple-element.18), channel_id=1, source_target_pairs={{0,16},{1,241},{2,18},{3,243},{4,20},{5,245},{6,22},{7,247},{8,24}... | collective-permute-start | bytes 835592 | tf_op jit(solution)/shard_map/ppermute | solution.py:219
  76.7 11.7 %collective-permute-start.5 = (f32[2,2,17,8,128]{4,3,2,1,0:T(8,128)S(1)}, f32[2,2,17,8,128]{4,3,2,1,0:T(8,128)S(1)}, u32[]{:S(2)}, u32[]{:S(2)}) collective-permute-start(f32[2,2,17,8,128]{4,3,2,1,0:T(8,128)S(1)} %get-tuple-element.19), channel_id=1, source_target_pairs={{0,240},{1,17},{2,242},{3,19},{4,244},{5,21},{6,246},{7,23},{8,248... | collective-permute-start | bytes 835592 | tf_op jit(solution)/shard_map/ppermute | solution.py:219
  78.6 9.7 %collective-permute-start.6 = (f32[1,2,17,8,128]{4,3,2,1,0:T(8,128)S(1)}, f32[1,2,17,8,128]{4,3,2,1,0:T(8,128)S(1)}, u32[]{:S(2)}, u32[]{:S(2)}) collective-permute-start(f32[1,2,17,8,128]{4,3,2,1,0:T(8,128)S(1)} %get-tuple-element.20), channel_id=1, source_target_pairs={{0,32},{1,225},{2,34},{3,227},{4,36},{5,229},{6,38},{7,231},{8,40}... | collective-permute-start | bytes 417800 | tf_op jit(solution)/shard_map/ppermute | solution.py:219
  92.9 4.1 %collective-permute-start.9 = (f32[8,16,1024]{2,1,0:T(8,128)S(1)}, f32[8,16,1024]{2,1,0:T(8,128)S(1)}, u32[]{:S(2)}, u32[]{:S(2)}) collective-permute-start(f32[8,16,1024]{2,1,0:T(8,128)S(1)} %get-tuple-element.28), channel_id=1, source_target_pairs={{0,1},{1,0},{2,3},{3,2},{4,5},{5,4},{6,7},{7,6},{8,9},{9,8},{10,11... | collective-permute-start | bytes 1572872 | tf_op jit(solution)/shard_map/ppermute | solution.py:201

commit v4 on v3

--- a/solution.py
+++ b/solution.py
@@ -190,7 +190,7 @@
         scratch_shapes=[pltpu.VMEM((width, 2 * padded), jnp.bfloat16)],
         compiler_params=pltpu.CompilerParams(vmem_limit_bytes=24 * 1024 * 1024),
         cost_estimate=pl.CostEstimate(
-            flops=6 * rows * width * ab, bytes_accessed=4 * ab * width, transcendentals=0
+            flops=rows * width * ab // 8, bytes_accessed=ab * width, transcendentals=0
         ),
     )(scal, *sources, w_hi, w_lo, *old)
 

time: 122 us -> 113 us (0.926)
  waiting for transfers between devices: 26.5 us -> 16.7 us
    ppermute x9, waiting for transfers between devices: 25 us -> 15.2 us  [move(): return lax.ppermute(array, ('vp', 'cd'), pairs)]
    ppermute x1, starting transfers between devices: 2.59 us -> 5.59 us  [reduce_rows(): both = mine + lax.ppermute(other, 'cd', pair)]
    ppermute x9, starting transfers between devices: 47.2 us -> 44.7 us  [move(): return lax.ppermute(array, ('vp', 'cd'), pairs)]
  transfers between devices with their start and end apart: 10 -> 10, of which waited for: 5 -> 3; matrix products, arithmetic and copies ran while one was open for 0% -> 0% of each run, Pallas kernels for 9% -> 10%
where the time goes in v4:
time: 113 us; the launch traced here: 112 us
  starting transfers between devices  50.3 us (45%)
  blocking collectives  23.2 us (21%)
  waiting for transfers between devices  16.7 us (15%)
  Pallas kernels  15.7 us (14%)
  local copies, waits for them, and re-layouts  4.93 us (4%)
    ppermute x9, starting transfers between devices, move(): return lax.ppermute(array, ('vp', 'cd'), pairs)  44.7 us
    all_to_all x1, blocking collectives, reduce_rows(): parts = lax.all_to_all(both, 'cd', 0, 0, axis_index_groups=groups)  23.2 us
    ppermute x9, waiting for transfers between devices, move(): return lax.ppermute(array, ('vp', 'cd'), pairs)  15.2 us
    pallas_call x2, Pallas kernels, contract(): pl.pallas_call(functools.partial(contract_kernel, rels, shapes, bool(old)...  11.2 us
    ppermute x1, starting transfers between devices, reduce_rows(): both = mine + lax.ppermute(other, 'cd', pair)  5.59 us
    unnamed x8, local copies, waits for them, and re-layouts  4.93 us
    pallas_call x1, Pallas kernels, prepare(): pl.pallas_call(functools.partial(prepare_kernel, owners, width // LANES +...  3.33 us
  transfers between devices with their start and end apart: 10, of which 3 were waited for; matrix products, arithmetic and copies ran while one was open for 0% of the time, Pallas kernels for 10%

profile of v4, /device:TPU:1, one launch (start us, length us, event | category | flops | bytes accessed | tf_op | source)
XLA Modules:
  0.0 111.8 jit_solution(14929972807739348154)
XLA Ops:
  0.0 18.7 %collective-permute-start = (f32[2,32,8,128]{3,2,1,0:T(8,128)}, f32[2,32,8,128]{3,2,1,0:T(8,128)S(1)}, u32[]{:S(2)}, u32[]{:S(2)}) collective-permute-start(f32[2,32,8,128]{3,2,1,0:T(8,128)} %bitcast.5), channel_id=1, source_target_pairs={{0,48},{1,209},{2,50},{3,211},{4,52},{5,213},{6,54},{7,215},{8,56}... | collective-permute-start | bytes 786440 | tf_op jit(solution)/shard_map/ppermute | solution.py:219
  18.7 1.9 %collective-permute-start.2 = (f32[2,32,8,128]{3,2,1,0:T(8,128)}, f32[2,32,8,128]{3,2,1,0:T(8,128)S(1)}, u32[]{:S(2)}, u32[]{:S(2)}) collective-permute-start(f32[2,32,8,128]{3,2,1,0:T(8,128)} %bitcast.6), channel_id=1, source_target_pairs={{0,208},{1,49},{2,210},{3,51},{4,212},{5,53},{6,214},{7,55},{8,216... | collective-permute-start | bytes 786440 | tf_op jit(solution)/shard_map/ppermute | solution.py:219
  20.7 14.4 %collective-permute-done.refs_1_ = f32[2,32,8,128]{3,2,1,0:T(8,128)S(1)} collective-permute-done((f32[2,32,8,128]{3,2,1,0:T(8,128)}, f32[2,32,8,128]{3,2,1,0:T(8,128)S(1)}, u32[]{:S(2)}, u32[]{:S(2)}) %collective-permute-start) | collective-permute-done | bytes 262176 | tf_op jit(solution)/shard_map/ppermute | solution.py:219
  35.0 7.1 %collective-permute-start.1 = (f32[2,32,8,128]{3,2,1,0:T(8,128)S(1)}, f32[2,32,8,128]{3,2,1,0:T(8,128)S(1)}, u32[]{:S(2)}, u32[]{:S(2)}) collective-permute-start(f32[2,32,8,128]{3,2,1,0:T(8,128)S(1)} %collective-permute-done.refs_1_), channel_id=1, source_target_pairs={{0,48},{1,209},{2,50},{3,211},{4,52},{5,213},{6,54},{7,215},{8,56}... | collective-permute-start | bytes 786440 | tf_op jit(solution)/shard_map/ppermute | solution.py:219
  42.2 0.0 collective-permute-done.2.refs_2_
  42.2 1.9 %collective-permute-start.3 = (f32[2,32,8,128]{3,2,1,0:T(8,128)S(1)}, f32[2,32,8,128]{3,2,1,0:T(8,128)S(1)}, u32[]{:S(2)}, u32[]{:S(2)}) collective-permute-start(f32[2,32,8,128]{3,2,1,0:T(8,128)S(1)} %collective-permute-done.2.refs_2_), channel_id=1, source_target_pairs={{0,208},{1,49},{2,210},{3,51},{4,212},{5,53},{6,214},{7,55},{8,216... | collective-permute-start | bytes 786440 | tf_op jit(solution)/shard_map/ppermute | solution.py:219
  44.1 0.0 copy-start
  44.1 3.4 %copy-done = f32[1024,2048]{1,0:T(8,128)S(1)} copy-done((f32[1024,2048]{1,0:T(8,128)S(1)}, f32[1024,2048]{1,0:T(8,128)}, u32[]{:S(2)}) %copy-start) | copy-done | bytes 8388632
  47.5 0.0 copy-start.2
  47.5 0.8 copy-done.2
  48.4 0.0 copy-start.3
  48.4 0.7 copy-done.3
  49.1 0.0 copy-start.1
  49.1 3.3 %shard_map.46 = (s32[16]{0:T(128)S(1)}, bf16[1024,2048]{1,0:T(8,128)(2,1)S(1)}, bf16[1024,2048]{1,0:T(8,128)(2,1)S(1)}) custom-call(s32[128,128]{1,0:T(8,128)S(1)} %bitcast.9, s32[32,128]{1,0:T(8,128)S(1)} %bitcast.10, f32[1024,2048]{1,0:T(8,128)S(1)} %copy-done), custom_call_target="tpu_custom_call" | custom-call | flops 16777216 | bytes 16777216 | tf_op jit(solution)/shard_map/pallas_call | solution.py:77
  52.4 0.0 copy-done.1
  52.4 0.6 shard_map.48
  53.0 1.9 %collective-permute-start.7 = (f32[3,2,17,8,128]{4,3,2,1,0:T(8,128)S(1)}, f32[3,2,17,8,128]{4,3,2,1,0:T(8,128)S(1)}, u32[]{:S(2)}, u32[]{:S(2)}) collective-permute-start(f32[3,2,17,8,128]{4,3,2,1,0:T(8,128)S(1)} %get-tuple-element.23), channel_id=1, source_target_pairs={{0,16},{1,241},{2,18},{3,243},{4,20},{5,245},{6,22},{7,247},{8,24}... | collective-permute-start | bytes 1253384 | tf_op jit(solution)/shard_map/ppermute | solution.py:219
  55.0 3.4 %collective-permute-start.8 = (f32[3,2,17,8,128]{4,3,2,1,0:T(8,128)S(1)}, f32[3,2,17,8,128]{4,3,2,1,0:T(8,128)S(1)}, u32[]{:S(2)}, u32[]{:S(2)}) collective-permute-start(f32[3,2,17,8,128]{4,3,2,1,0:T(8,128)S(1)} %get-tuple-element.24), channel_id=1, source_target_pairs={{0,240},{1,17},{2,242},{3,19},{4,244},{5,21},{6,246},{7,23},{8,248... | collective-permute-start | bytes 1253384 | tf_op jit(solution)/shard_map/ppermute | solution.py:219
  58.3 0.0 collective-permute-done.1.refs_0_.refs_3_
  58.3 0.8 collective-permute-done.3.refs_1_.refs_4_
  59.1 0.6 shard_map.47
  59.7 2.4 %collective-permute-start.4 = (f32[2,2,17,8,128]{4,3,2,1,0:T(8,128)S(1)}, f32[2,2,17,8,128]{4,3,2,1,0:T(8,128)S(1)}, u32[]{:S(2)}, u32[]{:S(2)}) collective-permute-start(f32[2,2,17,8,128]{4,3,2,1,0:T(8,128)S(1)} %get-tuple-element.18), channel_id=1, source_target_pairs={{0,16},{1,241},{2,18},{3,243},{4,20},{5,245},{6,22},{7,247},{8,24}... | collective-permute-start | bytes 835592 | tf_op jit(solution)/shard_map/ppermute | solution.py:219
  62.1 2.9 %collective-permute-start.5 = (f32[2,2,17,8,128]{4,3,2,1,0:T(8,128)S(1)}, f32[2,2,17,8,128]{4,3,2,1,0:T(8,128)S(1)}, u32[]{:S(2)}, u32[]{:S(2)}) collective-permute-start(f32[2,2,17,8,128]{4,3,2,1,0:T(8,128)S(1)} %get-tuple-element.19), channel_id=1, source_target_pairs={{0,240},{1,17},{2,242},{3,19},{4,244},{5,21},{6,246},{7,23},{8,248... | collective-permute-start | bytes 835592 | tf_op jit(solution)/shard_map/ppermute | solution.py:219
  65.0 4.4 %collective-permute-start.6 = (f32[1,2,17,8,128]{4,3,2,1,0:T(8,128)S(1)}, f32[1,2,17,8,128]{4,3,2,1,0:T(8,128)S(1)}, u32[]{:S(2)}, u32[]{:S(2)}) collective-permute-start(f32[1,2,17,8,128]{4,3,2,1,0:T(8,128)S(1)} %get-tuple-element.20), channel_id=1, source_target_pairs={{0,32},{1,225},{2,34},{3,227},{4,36},{5,229},{6,38},{7,231},{8,40}... | collective-permute-start | bytes 417800 | tf_op jit(solution)/shard_map/ppermute | solution.py:219
  69.5 0.0 collective-permute-done.7.refs_5_
  69.5 0.0 collective-permute-done.8.refs_6_
  69.5 6.6 %shard_map.49 = (f32[8,16,1024]{2,1,0:T(8,128)S(1)}, f32[8,16,1024]{2,1,0:T(8,128)S(1)}) custom-call(s32[16]{0:T(128)S(1)} %get-tuple-element.17.scal, f32[2,32,8,128]{3,2,1,0:T(8,128)S(1)} %bitcast.8, f32[2,32,8,128]{3,2,1,0:T(8,128)S(1)} %collective-permute-done.refs_1_, f32[2,32,8,128]{3,2,1,0:T(8,128)S(1)} %collective-permute-done.2.refs_2_, ...), custom_call_target="tpu_custom_call" | custom-call | flops 46137344 | bytes 2097152 | tf_op jit(solution)/shard_map/pallas_call | solution.py:184
  76.1 0.0 collective-permute-done.6.refs_2_
  76.1 0.0 collective-permute-done.4.refs_0_
  76.1 0.0 collective-permute-done.5.refs_1_
  76.1 4.6 %shard_map.50 = (f32[8,16,1024]{2,1,0:T(8,128)S(1)}, f32[8,16,1024]{2,1,0:T(8,128)S(1)}) custom-call(s32[16]{0:T(128)S(1)} %get-tuple-element.17.scal, f32[2,2,17,8,128]{4,3,2,1,0:T(8,128)S(1)} %collective-permute-done.4.refs_0_, f32[2,2,17,8,128]{4,3,2,1,0:T(8,128)S(1)} %collective-permute-done.5.refs_1_, ...), custom_call_target="tpu_custom_call" | custom-call | flops 20971520 | bytes 2097152 | tf_op jit(solution)/shard_map/pallas_call | solution.py:184
  80.7 5.6 %collective-permute-start.9 = (f32[8,16,1024]{2,1,0:T(8,128)S(1)}, f32[8,16,1024]{2,1,0:T(8,128)S(1)}, u32[]{:S(2)}, u32[]{:S(2)}) collective-permute-start(f32[8,16,1024]{2,1,0:T(8,128)S(1)} %get-tuple-element.28), channel_id=1, source_target_pairs={{0,1},{1,0},{2,3},{3,2},{4,5},{5,4},{6,7},{7,6},{8,9},{9,8},{10,11... | collective-permute-start | bytes 1572872 | tf_op jit(solution)/shard_map/ppermute | solution.py:201
  86.3 1.5 %collective-permute-done.9 = f32[8,16,1024]{2,1,0:T(8,128)S(1)} collective-permute-done((f32[8,16,1024]{2,1,0:T(8,128)S(1)}, f32[8,16,1024]{2,1,0:T(8,128)S(1)}, u32[]{:S(2)}, u32[]{:S(2)}) %collective-permute-start.9) | collective-permute-done | bytes 524320 | tf_op jit(solution)/shard_map/ppermute | solution.py:201
  87.8 0.1 add.3
  87.9 23.2 %all_to_all.5 = f32[8,16,1024]{2,1,0:T(8,128)S(1)} all-to-all(f32[8,16,1024]{2,1,0:T(8,128)S(1)} %add.3), channel_id=1, replica_groups={{0,2,4,6,8,10,12,14},{1,3,5,7,9,11,13,15},{16,18,20,22,24,26,28,30},{17..., dimensions={0} | all-to-all | bytes 1048576 | tf_op jit(solution)/shard_map/all_to_all | solution.py:203
  111.1 0.7 reduce_sum.9
Async XLA Ops:
  0.0 35.0 %collective-permute-start = (f32[2,32,8,128]{3,2,1,0:T(8,128)}, f32[2,32,8,128]{3,2,1,0:T(8,128)S(1)}, u32[]{:S(2)}, u32[]{:S(2)}) collective-permute-start(f32[2,32,8,128]{3,2,1,0:T(8,128)} %bitcast.5), channel_id=1, source_target_pairs={{0,48},{1,209},{2,50},{3,211},{4,52},{5,213},{6,54},{7,215},{8,56}... | collective-permute-start | bytes 786440 | tf_op jit(solution)/shard_map/ppermute | solution.py:219
  18.7 23.4 %collective-permute-start.2 = (f32[2,32,8,128]{3,2,1,0:T(8,128)}, f32[2,32,8,128]{3,2,1,0:T(8,128)S(1)}, u32[]{:S(2)}, u32[]{:S(2)}) collective-permute-start(f32[2,32,8,128]{3,2,1,0:T(8,128)} %bitcast.6), channel_id=1, source_target_pairs={{0,208},{1,49},{2,210},{3,51},{4,212},{5,53},{6,214},{7,55},{8,216... | collective-permute-start | bytes 786440 | tf_op jit(solution)/shard_map/ppermute | solution.py:219
  35.0 23.3 %collective-permute-start.1 = (f32[2,32,8,128]{3,2,1,0:T(8,128)S(1)}, f32[2,32,8,128]{3,2,1,0:T(8,128)S(1)}, u32[]{:S(2)}, u32[]{:S(2)}) collective-permute-start(f32[2,32,8,128]{3,2,1,0:T(8,128)S(1)} %collective-permute-done.refs_1_), channel_id=1, source_target_pairs={{0,48},{1,209},{2,50},{3,211},{4,52},{5,213},{6,54},{7,215},{8,56}... | collective-permute-start | bytes 786440 | tf_op jit(solution)/shard_map/ppermute | solution.py:219
  42.2 16.9 %collective-permute-start.3 = (f32[2,32,8,128]{3,2,1,0:T(8,128)S(1)}, f32[2,32,8,128]{3,2,1,0:T(8,128)S(1)}, u32[]{:S(2)}, u32[]{:S(2)}) collective-permute-start(f32[2,32,8,128]{3,2,1,0:T(8,128)S(1)} %collective-permute-done.2.refs_2_), channel_id=1, source_target_pairs={{0,208},{1,49},{2,210},{3,51},{4,212},{5,53},{6,214},{7,55},{8,216... | collective-permute-start | bytes 786440 | tf_op jit(solution)/shard_map/ppermute | solution.py:219
  44.1 3.4 %copy-start = (f32[1024,2048]{1,0:T(8,128)S(1)}, f32[1024,2048]{1,0:T(8,128)}, u32[]{:S(2)}) copy-start(f32[1024,2048]{1,0:T(8,128)} %w_ref.1) | copy-start | bytes 25165828
  47.5 0.8 copy-start.2
  48.4 0.7 copy-start.3
  49.1 3.3 %copy-start.1 = (f32[16,4096]{1,0:T(8,128)S(1)}, f32[16,4096]{1,0:T(8,128)}, u32[]{:S(2)}) copy-start(f32[16,4096]{1,0:T(8,128)} %param.4) | copy-start | bytes 786436
  53.0 16.4 %collective-permute-start.7 = (f32[3,2,17,8,128]{4,3,2,1,0:T(8,128)S(1)}, f32[3,2,17,8,128]{4,3,2,1,0:T(8,128)S(1)}, u32[]{:S(2)}, u32[]{:S(2)}) collective-permute-start(f32[3,2,17,8,128]{4,3,2,1,0:T(8,128)S(1)} %get-tuple-element.23), channel_id=1, source_target_pairs={{0,16},{1,241},{2,18},{3,243},{4,20},{5,245},{6,22},{7,247},{8,24}... | collective-permute-start | bytes 1253384 | tf_op jit(solution)/shard_map/ppermute | solution.py:219
  55.0 14.5 %collective-permute-start.8 = (f32[3,2,17,8,128]{4,3,2,1,0:T(8,128)S(1)}, f32[3,2,17,8,128]{4,3,2,1,0:T(8,128)S(1)}, u32[]{:S(2)}, u32[]{:S(2)}) collective-permute-start(f32[3,2,17,8,128]{4,3,2,1,0:T(8,128)S(1)} %get-tuple-element.24), channel_id=1, source_target_pairs={{0,240},{1,17},{2,242},{3,19},{4,244},{5,21},{6,246},{7,23},{8,248... | collective-permute-start | bytes 1253384 | tf_op jit(solution)/shard_map/ppermute | solution.py:219
  59.7 16.4 %collective-permute-start.4 = (f32[2,2,17,8,128]{4,3,2,1,0:T(8,128)S(1)}, f32[2,2,17,8,128]{4,3,2,1,0:T(8,128)S(1)}, u32[]{:S(2)}, u32[]{:S(2)}) collective-permute-start(f32[2,2,17,8,128]{4,3,2,1,0:T(8,128)S(1)} %get-tuple-element.18), channel_id=1, source_target_pairs={{0,16},{1,241},{2,18},{3,243},{4,20},{5,245},{6,22},{7,247},{8,24}... | collective-permute-start | bytes 835592 | tf_op jit(solution)/shard_map/ppermute | solution.py:219
  62.1 14.0 %collective-permute-start.5 = (f32[2,2,17,8,128]{4,3,2,1,0:T(8,128)S(1)}, f32[2,2,17,8,128]{4,3,2,1,0:T(8,128)S(1)}, u32[]{:S(2)}, u32[]{:S(2)}) collective-permute-start(f32[2,2,17,8,128]{4,3,2,1,0:T(8,128)S(1)} %get-tuple-element.19), channel_id=1, source_target_pairs={{0,240},{1,17},{2,242},{3,19},{4,244},{5,21},{6,246},{7,23},{8,248... | collective-permute-start | bytes 835592 | tf_op jit(solution)/shard_map/ppermute | solution.py:219
  65.0 11.1 %collective-permute-start.6 = (f32[1,2,17,8,128]{4,3,2,1,0:T(8,128)S(1)}, f32[1,2,17,8,128]{4,3,2,1,0:T(8,128)S(1)}, u32[]{:S(2)}, u32[]{:S(2)}) collective-permute-start(f32[1,2,17,8,128]{4,3,2,1,0:T(8,128)S(1)} %get-tuple-element.20), channel_id=1, source_target_pairs={{0,32},{1,225},{2,34},{3,227},{4,36},{5,229},{6,38},{7,231},{8,40}... | collective-permute-start | bytes 417800 | tf_op jit(solution)/shard_map/ppermute | solution.py:219
  80.7 7.1 %collective-permute-start.9 = (f32[8,16,1024]{2,1,0:T(8,128)S(1)}, f32[8,16,1024]{2,1,0:T(8,128)S(1)}, u32[]{:S(2)}, u32[]{:S(2)}) collective-permute-start(f32[8,16,1024]{2,1,0:T(8,128)S(1)} %get-tuple-element.28), channel_id=1, source_target_pairs={{0,1},{1,0},{2,3},{3,2},{4,5},{5,4},{6,7},{7,6},{8,9},{9,8},{10,11... | collective-permute-start | bytes 1572872 | tf_op jit(solution)/shard_map/ppermute | solution.py:201

commit v5 on v4

--- a/solution.py
+++ b/solution.py
@@ -9,6 +9,7 @@
 
 LANES = 128
 AB_TILE = 256
+CONTRACT_TILE = 1024
 IRREPS = 8
 OFF, N_LOW, COL0, COL1, COL2, TILE = 0, 1, 2, 3, 4, 5
 
@@ -85,7 +86,7 @@
         out_specs=[pl.BlockSpec(memory_space=pltpu.SMEM), tile_spec, tile_spec],
         out_shape=[jax.ShapeDtypeStruct((16,), jnp.int32), half, half],
         scratch_shapes=[pltpu.SMEM((16,), jnp.int32)],
-        compiler_params=pltpu.CompilerParams(vmem_limit_bytes=24 * 1024 * 1024),
+        compiler_params=pltpu.CompilerParams(vmem_limit_bytes=16 * 1024 * 1024),
         cost_estimate=pl.CostEstimate(flops=8 * ab * width, bytes_accessed=8 * ab * width, transcendentals=0),
     )(labels_ab, labels_cd, w_slab)
 
@@ -118,57 +119,54 @@
     srcs, refs = refs[:n_src], refs[n_src:]
     w_hi, w_lo, refs = refs[0], refs[1], refs[2:]
     if carried:
-        old_mine, old_other, refs = refs[0], refs[1], refs[2:]
+        refs = refs[2:]
     mine, other, amps = refs
     width = w_hi.shape[1]
     padded = amps.shape[1] // 2
     tiles = width // LANES
     share = mine.shape[1]
 
-    @pl.when(pl.program_id(0) == 0)
-    def build():
-        off, tile0 = scal[OFF], scal[TILE]
-        lane = lax.broadcasted_iota(jnp.int32, (padded, LANES), 1)
-        keep = lane < LANES - off
-        turn = lax.rem(LANES - off, LANES)
-        rolled = None
-        for j in range(tiles + 1):
-            pieces = []
-            for ref, count in zip(srcs, shapes):
-                if count is None:
-                    pieces.append(ref[:, pl.ds(tile0 + j, 1)].reshape(share, LANES))
-                else:
-                    pieces += [ref[i, :, j].reshape(share, LANES) for i in range(count)]
-            if padded > share * len(rels):
-                pieces.append(jnp.zeros((padded - share * len(rels), LANES), jnp.float32))
-            new = pltpu.roll(jnp.concatenate(pieces, axis=0), turn, 1)
-            if rolled is not None:
-                value = jnp.where(keep, rolled, new).T
-                high = value.astype(jnp.bfloat16)
-                rows = slice((j - 1) * LANES, j * LANES)
-                amps[rows, :padded] = high
-                amps[rows, padded:] = (value - high.astype(jnp.float32)).astype(jnp.bfloat16)
-            rolled = new
+    off, tile0 = scal[OFF], scal[TILE]
+    lane = lax.broadcasted_iota(jnp.int32, (padded, LANES), 1)
+    keep = lane < LANES - off
+    turn = lax.rem(LANES - off, LANES)
+    rolled = None
+    for j in range(tiles + 1):
+        pieces = []
+        for ref, count in zip(srcs, shapes):
+            if count is None:
+                pieces.append(ref[:, pl.ds(tile0 + j, 1)].reshape(share, LANES))
+            else:
+                pieces += [ref[i, :, j].reshape(share, LANES) for i in range(count)]
+        if padded > share * len(rels):
+            pieces.append(jnp.zeros((padded - share * len(rels), LANES), jnp.float32))
+        new = pltpu.roll(jnp.concatenate(pieces, axis=0), turn, 1)
+        if rolled is not None:
+            value = jnp.where(keep, rolled, new).T
+            high = value.astype(jnp.bfloat16)
+            rows = slice((j - 1) * LANES, j * LANES)
+            amps[rows, :padded] = high
+            amps[rows, padded:] = (value - high.astype(jnp.float32)).astype(jnp.bfloat16)
+        rolled = new
 
     dot = functools.partial(jnp.dot, preferred_element_type=jnp.float32)
-    both = dot(w_hi[...], amps[...])
-    turned = both[:, :padded] + both[:, padded:] + dot(w_lo[...], amps[:, :padded])
-    out = turned.T
-    if carried:
-        mine[...] = old_mine[...]
-        other[...] = old_other[...]
     z, core, d = position()
-    for i, rel in enumerate(rels):
-        block = (z + rel * d + 32) & 15
-        value = out[i * share : (i + 1) * share]
-
-        @pl.when((block & 1) == core)
-        def keep_block():
-            mine[pl.ds(block >> 1, 1)] = value[None]
-
-        @pl.when((block & 1) != core)
-        def send_block():
-            other[pl.ds(block >> 1, 1)] = value[None]
+    for at in range(0, w_hi.shape[0], CONTRACT_TILE):
+        cols = slice(at, at + CONTRACT_TILE)
+        both = dot(w_hi[cols], amps[...])
+        turned = both[:, :padded] + both[:, padded:] + dot(w_lo[cols], amps[:, :padded])
+        out = turned.T
+        for i, rel in enumerate(rels):
+            block = (z + rel * d + 32) & 15
+            value = out[i * share : (i + 1) * share]
+
+            @pl.when((block & 1) == core)
+            def keep_block():
+                mine[pl.ds(block >> 1, 1), :, cols] = value[None]
+
+            @pl.when((block & 1) != core)
+            def send_block():
+                other[pl.ds(block >> 1, 1), :, cols] = value[None]
 
 
 def contract(scal, sources, rels, w_hi, w_lo, old=()):
@@ -177,18 +175,17 @@
     share = 16
     rows = share * len(rels)
     padded = -(-rows // LANES) * LANES
-    whole = [pl.BlockSpec(s.shape, functools.partial(lambda n, i: (0,) * n, s.ndim)) for s in sources]
-    tile_spec = pl.BlockSpec((AB_TILE, width), lambda i: (i, 0))
-    out_spec = pl.BlockSpec((8, share, AB_TILE), lambda i: (0, 0, i))
+    vmem = pl.BlockSpec(memory_space=pltpu.VMEM)
     out_shape = jax.ShapeDtypeStruct((8, share, ab), jnp.float32)
+    n_in = len(sources) + 3
     return pl.pallas_call(
         functools.partial(contract_kernel, rels, shapes, bool(old)),
-        grid=(ab // AB_TILE,),
-        in_specs=[pl.BlockSpec(memory_space=pltpu.SMEM)] + whole + [tile_spec] * 2 + [out_spec] * len(old),
-        out_specs=[out_spec, out_spec],
+        in_specs=[pl.BlockSpec(memory_space=pltpu.SMEM)] + [vmem] * (n_in - 1 + len(old)),
+        out_specs=[vmem, vmem],
         out_shape=[out_shape, out_shape],
+        input_output_aliases={n_in: 0, n_in + 1: 1} if old else {},
         scratch_shapes=[pltpu.VMEM((width, 2 * padded), jnp.bfloat16)],
-        compiler_params=pltpu.CompilerParams(vmem_limit_bytes=24 * 1024 * 1024),
+        compiler_params=pltpu.CompilerParams(vmem_limit_bytes=20 * 1024 * 1024),
         cost_estimate=pl.CostEstimate(
             flops=rows * width * ab // 8, bytes_accessed=ab * width, transcendentals=0
         ),

time: 113 us -> 111 us (0.982)
  Pallas kernels: 15.7 us -> 12.3 us
  starting transfers between devices: 50.3 us -> 51.6 us
    pallas_call x2, Pallas kernels: 11.2 us -> 7.8 us  [contract(): pl.pallas_call(functools.partial(contract_kernel, rels, shapes, bool(old)...]
    ppermute x1, starting transfers between devices: 5.59 us -> 6.84 us  [reduce_rows(): both = mine + lax.ppermute(other, 'cd', pair)]
  transfers between devices with their start and end apart: 10 -> 10, of which waited for: 3 -> 4; matrix products, arithmetic and copies ran while one was open for 0% -> 0% of each run, Pallas kernels for 10% -> 8%
where the time goes in v5:
time: 111 us; the launch traced here: 110 us
  starting transfers between devices  51.6 us (46%)
  blocking collectives  23.2 us (21%)
  waiting for transfers between devices  17.5 us (16%)
  Pallas kernels  12.3 us (11%)
  local copies, waits for them, and re-layouts  4.93 us (4%)
    ppermute x9, starting transfers between devices, move(): return lax.ppermute(array, ('vp', 'cd'), pairs)  44.7 us
    all_to_all x1, blocking collectives, reduce_rows(): parts = lax.all_to_all(both, 'cd', 0, 0, axis_index_groups=groups)  23.2 us
    ppermute x9, waiting for transfers between devices, move(): return lax.ppermute(array, ('vp', 'cd'), pairs)  16 us
    pallas_call x2, Pallas kernels, contract(): pl.pallas_call(functools.partial(contract_kernel, rels, shapes, bool(old)...  7.8 us
    ppermute x1, starting transfers between devices, reduce_rows(): both = mine + lax.ppermute(other, 'cd', pair)  6.84 us
    unnamed x8, local copies, waits for them, and re-layouts  4.93 us
    pallas_call x1, Pallas kernels, prepare(): pl.pallas_call(functools.partial(prepare_kernel, owners, width // LANES +...  3.33 us
  transfers between devices with their start and end apart: 10, of which 4 were waited for; matrix products, arithmetic and copies ran while one was open for 0% of the time, Pallas kernels for 8%

profile of v5, /device:TPU:1, one launch (start us, length us, event | category | flops | bytes accessed | tf_op | source)
XLA Modules:
  0.0 110.5 jit_solution(15101075191180131529)
XLA Ops:
  0.0 18.7 %collective-permute-start = (f32[2,32,8,128]{3,2,1,0:T(8,128)}, f32[2,32,8,128]{3,2,1,0:T(8,128)S(1)}, u32[]{:S(2)}, u32[]{:S(2)}) collective-permute-start(f32[2,32,8,128]{3,2,1,0:T(8,128)} %bitcast.5), channel_id=1, source_target_pairs={{0,48},{1,209},{2,50},{3,211},{4,52},{5,213},{6,54},{7,215},{8,56}... | collective-permute-start | bytes 786440 | tf_op jit(solution)/shard_map/ppermute | solution.py:216
  18.7 1.9 %collective-permute-start.2 = (f32[2,32,8,128]{3,2,1,0:T(8,128)}, f32[2,32,8,128]{3,2,1,0:T(8,128)S(1)}, u32[]{:S(2)}, u32[]{:S(2)}) collective-permute-start(f32[2,32,8,128]{3,2,1,0:T(8,128)} %bitcast.6), channel_id=1, source_target_pairs={{0,208},{1,49},{2,210},{3,51},{4,212},{5,53},{6,214},{7,55},{8,216... | collective-permute-start | bytes 786440 | tf_op jit(solution)/shard_map/ppermute | solution.py:216
  20.7 14.4 %collective-permute-done.refs_1_ = f32[2,32,8,128]{3,2,1,0:T(8,128)S(1)} collective-permute-done((f32[2,32,8,128]{3,2,1,0:T(8,128)}, f32[2,32,8,128]{3,2,1,0:T(8,128)S(1)}, u32[]{:S(2)}, u32[]{:S(2)}) %collective-permute-start) | collective-permute-done | bytes 262176 | tf_op jit(solution)/shard_map/ppermute | solution.py:216
  35.0 7.1 %collective-permute-start.1 = (f32[2,32,8,128]{3,2,1,0:T(8,128)S(1)}, f32[2,32,8,128]{3,2,1,0:T(8,128)S(1)}, u32[]{:S(2)}, u32[]{:S(2)}) collective-permute-start(f32[2,32,8,128]{3,2,1,0:T(8,128)S(1)} %collective-permute-done.refs_1_), channel_id=1, source_target_pairs={{0,48},{1,209},{2,50},{3,211},{4,52},{5,213},{6,54},{7,215},{8,56}... | collective-permute-start | bytes 786440 | tf_op jit(solution)/shard_map/ppermute | solution.py:216
  42.2 0.0 collective-permute-done.2.refs_2_
  42.2 1.9 %collective-permute-start.3 = (f32[2,32,8,128]{3,2,1,0:T(8,128)S(1)}, f32[2,32,8,128]{3,2,1,0:T(8,128)S(1)}, u32[]{:S(2)}, u32[]{:S(2)}) collective-permute-start(f32[2,32,8,128]{3,2,1,0:T(8,128)S(1)} %collective-permute-done.2.refs_2_), channel_id=1, source_target_pairs={{0,208},{1,49},{2,210},{3,51},{4,212},{5,53},{6,214},{7,55},{8,216... | collective-permute-start | bytes 786440 | tf_op jit(solution)/shard_map/ppermute | solution.py:216
  44.1 0.0 copy-start
  44.1 3.4 %copy-done = f32[1024,2048]{1,0:T(8,128)S(1)} copy-done((f32[1024,2048]{1,0:T(8,128)S(1)}, f32[1024,2048]{1,0:T(8,128)}, u32[]{:S(2)}) %copy-start) | copy-done | bytes 8388632
  47.5 0.0 copy-start.2
  47.5 0.8 copy-done.2
  48.4 0.0 copy-start.3
  48.4 0.7 copy-done.3
  49.1 0.0 copy-start.1
  49.1 3.3 %shard_map.46 = (s32[16]{0:T(128)S(1)}, bf16[1024,2048]{1,0:T(8,128)(2,1)S(1)}, bf16[1024,2048]{1,0:T(8,128)(2,1)S(1)}) custom-call(s32[128,128]{1,0:T(8,128)S(1)} %bitcast.9, s32[32,128]{1,0:T(8,128)S(1)} %bitcast.10, f32[1024,2048]{1,0:T(8,128)S(1)} %copy-done), custom_call_target="tpu_custom_call" | custom-call | flops 16777216 | bytes 16777216 | tf_op jit(solution)/shard_map/pallas_call | solution.py:78
  52.4 0.0 copy-done.1
  52.4 0.6 shard_map.48
  53.0 1.9 %collective-permute-start.7 = (f32[3,2,17,8,128]{4,3,2,1,0:T(8,128)S(1)}, f32[3,2,17,8,128]{4,3,2,1,0:T(8,128)S(1)}, u32[]{:S(2)}, u32[]{:S(2)}) collective-permute-start(f32[3,2,17,8,128]{4,3,2,1,0:T(8,128)S(1)} %get-tuple-element.23), channel_id=1, source_target_pairs={{0,16},{1,241},{2,18},{3,243},{4,20},{5,245},{6,22},{7,247},{8,24}... | collective-permute-start | bytes 1253384 | tf_op jit(solution)/shard_map/ppermute | solution.py:216
  55.0 3.4 %collective-permute-start.8 = (f32[3,2,17,8,128]{4,3,2,1,0:T(8,128)S(1)}, f32[3,2,17,8,128]{4,3,2,1,0:T(8,128)S(1)}, u32[]{:S(2)}, u32[]{:S(2)}) collective-permute-start(f32[3,2,17,8,128]{4,3,2,1,0:T(8,128)S(1)} %get-tuple-element.24), channel_id=1, source_target_pairs={{0,240},{1,17},{2,242},{3,19},{4,244},{5,21},{6,246},{7,23},{8,248... | collective-permute-start | bytes 1253384 | tf_op jit(solution)/shard_map/ppermute | solution.py:216
  58.3 0.0 collective-permute-done.1.refs_0_.refs_3_
  58.3 0.8 collective-permute-done.3.refs_1_.refs_4_
  59.1 0.6 shard_map.47
  59.7 2.4 %collective-permute-start.4 = (f32[2,2,17,8,128]{4,3,2,1,0:T(8,128)S(1)}, f32[2,2,17,8,128]{4,3,2,1,0:T(8,128)S(1)}, u32[]{:S(2)}, u32[]{:S(2)}) collective-permute-start(f32[2,2,17,8,128]{4,3,2,1,0:T(8,128)S(1)} %get-tuple-element.18), channel_id=1, source_target_pairs={{0,16},{1,241},{2,18},{3,243},{4,20},{5,245},{6,22},{7,247},{8,24}... | collective-permute-start | bytes 835592 | tf_op jit(solution)/shard_map/ppermute | solution.py:216
  62.1 2.9 %collective-permute-start.5 = (f32[2,2,17,8,128]{4,3,2,1,0:T(8,128)S(1)}, f32[2,2,17,8,128]{4,3,2,1,0:T(8,128)S(1)}, u32[]{:S(2)}, u32[]{:S(2)}) collective-permute-start(f32[2,2,17,8,128]{4,3,2,1,0:T(8,128)S(1)} %get-tuple-element.19), channel_id=1, source_target_pairs={{0,240},{1,17},{2,242},{3,19},{4,244},{5,21},{6,246},{7,23},{8,248... | collective-permute-start | bytes 835592 | tf_op jit(solution)/shard_map/ppermute | solution.py:216
  65.0 4.4 %collective-permute-start.6 = (f32[1,2,17,8,128]{4,3,2,1,0:T(8,128)S(1)}, f32[1,2,17,8,128]{4,3,2,1,0:T(8,128)S(1)}, u32[]{:S(2)}, u32[]{:S(2)}) collective-permute-start(f32[1,2,17,8,128]{4,3,2,1,0:T(8,128)S(1)} %get-tuple-element.20), channel_id=1, source_target_pairs={{0,32},{1,225},{2,34},{3,227},{4,36},{5,229},{6,38},{7,231},{8,40}... | collective-permute-start | bytes 417800 | tf_op jit(solution)/shard_map/ppermute | solution.py:216
  69.5 0.0 collective-permute-done.7.refs_5_
  69.5 0.0 collective-permute-done.8.refs_6_
  69.5 4.5 %shard_map.49 = (f32[8,16,1024]{2,1,0:T(8,128)S(1)}, f32[8,16,1024]{2,1,0:T(8,128)S(1)}) custom-call(s32[16]{0:T(128)S(1)} %get-tuple-element.17.scal, f32[2,32,8,128]{3,2,1,0:T(8,128)S(1)} %bitcast.8, f32[2,32,8,128]{3,2,1,0:T(8,128)S(1)} %collective-permute-done.refs_1_, f32[2,32,8,128]{3,2,1,0:T(8,128)S(1)} %collective-permute-done.2.refs_2_, ...), custom_call_target="tpu_custom_call" | custom-call | flops 46137344 | bytes 2097152 | tf_op jit(solution)/shard_map/pallas_call | solution.py:181
  74.0 0.8 collective-permute-done.6.refs_2_
  74.9 0.0 collective-permute-done.4.refs_0_
  74.9 0.0 collective-permute-done.5.refs_1_
  74.9 3.3 %shard_map.50 = (f32[8,16,1024]{2,1,0:T(8,128)S(1)}, f32[8,16,1024]{2,1,0:T(8,128)S(1)}) custom-call(s32[16]{0:T(128)S(1)} %get-tuple-element.17.scal, f32[2,2,17,8,128]{4,3,2,1,0:T(8,128)S(1)} %collective-permute-done.4.refs_0_, f32[2,2,17,8,128]{4,3,2,1,0:T(8,128)S(1)} %collective-permute-done.5.refs_1_, ...), custom_call_target="tpu_custom_call", output_to_operand_aliasing={{0}: (6, {}), {1}: (7, {})} | custom-call | flops 20971520 | bytes 2097152 | tf_op jit(solution)/shard_map/pallas_call | solution.py:181
  78.1 6.8 %collective-permute-start.9 = (f32[8,16,1024]{2,1,0:T(8,128)S(1)}, f32[8,16,1024]{2,1,0:T(8,128)S(1)}, u32[]{:S(2)}, u32[]{:S(2)}) collective-permute-start(f32[8,16,1024]{2,1,0:T(8,128)S(1)} %get-tuple-element.28), channel_id=1, source_target_pairs={{0,1},{1,0},{2,3},{3,2},{4,5},{5,4},{6,7},{7,6},{8,9},{9,8},{10,11... | collective-permute-start | bytes 1572872 | tf_op jit(solution)/shard_map/ppermute | solution.py:198
  85.0 1.5 %collective-permute-done.9 = f32[8,16,1024]{2,1,0:T(8,128)S(1)} collective-permute-done((f32[8,16,1024]{2,1,0:T(8,128)S(1)}, f32[8,16,1024]{2,1,0:T(8,128)S(1)}, u32[]{:S(2)}, u32[]{:S(2)}) %collective-permute-start.9) | collective-permute-done | bytes 524320 | tf_op jit(solution)/shard_map/ppermute | solution.py:198
  86.5 0.1 add.3
  86.6 23.2 %all_to_all.5 = f32[8,16,1024]{2,1,0:T(8,128)S(1)} all-to-all(f32[8,16,1024]{2,1,0:T(8,128)S(1)} %add.3), channel_id=1, replica_groups={{0,2,4,6,8,10,12,14},{1,3,5,7,9,11,13,15},{16,18,20,22,24,26,28,30},{17..., dimensions={0} | all-to-all | bytes 1048576 | tf_op jit(solution)/shard_map/all_to_all | solution.py:200
  109.8 0.7 reduce_sum.9
Async XLA Ops:
  0.0 35.0 %collective-permute-start = (f32[2,32,8,128]{3,2,1,0:T(8,128)}, f32[2,32,8,128]{3,2,1,0:T(8,128)S(1)}, u32[]{:S(2)}, u32[]{:S(2)}) collective-permute-start(f32[2,32,8,128]{3,2,1,0:T(8,128)} %bitcast.5), channel_id=1, source_target_pairs={{0,48},{1,209},{2,50},{3,211},{4,52},{5,213},{6,54},{7,215},{8,56}... | collective-permute-start | bytes 786440 | tf_op jit(solution)/shard_map/ppermute | solution.py:216
  18.7 23.4 %collective-permute-start.2 = (f32[2,32,8,128]{3,2,1,0:T(8,128)}, f32[2,32,8,128]{3,2,1,0:T(8,128)S(1)}, u32[]{:S(2)}, u32[]{:S(2)}) collective-permute-start(f32[2,32,8,128]{3,2,1,0:T(8,128)} %bitcast.6), channel_id=1, source_target_pairs={{0,208},{1,49},{2,210},{3,51},{4,212},{5,53},{6,214},{7,55},{8,216... | collective-permute-start | bytes 786440 | tf_op jit(solution)/shard_map/ppermute | solution.py:216
  35.0 23.3 %collective-permute-start.1 = (f32[2,32,8,128]{3,2,1,0:T(8,128)S(1)}, f32[2,32,8,128]{3,2,1,0:T(8,128)S(1)}, u32[]{:S(2)}, u32[]{:S(2)}) collective-permute-start(f32[2,32,8,128]{3,2,1,0:T(8,128)S(1)} %collective-permute-done.refs_1_), channel_id=1, source_target_pairs={{0,48},{1,209},{2,50},{3,211},{4,52},{5,213},{6,54},{7,215},{8,56}... | collective-permute-start | bytes 786440 | tf_op jit(solution)/shard_map/ppermute | solution.py:216
  42.2 16.9 %collective-permute-start.3 = (f32[2,32,8,128]{3,2,1,0:T(8,128)S(1)}, f32[2,32,8,128]{3,2,1,0:T(8,128)S(1)}, u32[]{:S(2)}, u32[]{:S(2)}) collective-permute-start(f32[2,32,8,128]{3,2,1,0:T(8,128)S(1)} %collective-permute-done.2.refs_2_), channel_id=1, source_target_pairs={{0,208},{1,49},{2,210},{3,51},{4,212},{5,53},{6,214},{7,55},{8,216... | collective-permute-start | bytes 786440 | tf_op jit(solution)/shard_map/ppermute | solution.py:216
  44.1 3.4 %copy-start = (f32[1024,2048]{1,0:T(8,128)S(1)}, f32[1024,2048]{1,0:T(8,128)}, u32[]{:S(2)}) copy-start(f32[1024,2048]{1,0:T(8,128)} %w_ref.1) | copy-start | bytes 25165828
  47.5 0.8 copy-start.2
  48.4 0.7 copy-start.3
  49.1 3.3 %copy-start.1 = (f32[16,4096]{1,0:T(8,128)S(1)}, f32[16,4096]{1,0:T(8,128)}, u32[]{:S(2)}) copy-start(f32[16,4096]{1,0:T(8,128)} %param.4) | copy-start | bytes 786436
  53.0 16.4 %collective-permute-start.7 = (f32[3,2,17,8,128]{4,3,2,1,0:T(8,128)S(1)}, f32[3,2,17,8,128]{4,3,2,1,0:T(8,128)S(1)}, u32[]{:S(2)}, u32[]{:S(2)}) collective-permute-start(f32[3,2,17,8,128]{4,3,2,1,0:T(8,128)S(1)} %get-tuple-element.23), channel_id=1, source_target_pairs={{0,16},{1,241},{2,18},{3,243},{4,20},{5,245},{6,22},{7,247},{8,24}... | collective-permute-start | bytes 1253384 | tf_op jit(solution)/shard_map/ppermute | solution.py:216
  55.0 14.5 %collective-permute-start.8 = (f32[3,2,17,8,128]{4,3,2,1,0:T(8,128)S(1)}, f32[3,2,17,8,128]{4,3,2,1,0:T(8,128)S(1)}, u32[]{:S(2)}, u32[]{:S(2)}) collective-permute-start(f32[3,2,17,8,128]{4,3,2,1,0:T(8,128)S(1)} %get-tuple-element.24), channel_id=1, source_target_pairs={{0,240},{1,17},{2,242},{3,19},{4,244},{5,21},{6,246},{7,23},{8,248... | collective-permute-start | bytes 1253384 | tf_op jit(solution)/shard_map/ppermute | solution.py:216
  59.7 15.2 %collective-permute-start.4 = (f32[2,2,17,8,128]{4,3,2,1,0:T(8,128)S(1)}, f32[2,2,17,8,128]{4,3,2,1,0:T(8,128)S(1)}, u32[]{:S(2)}, u32[]{:S(2)}) collective-permute-start(f32[2,2,17,8,128]{4,3,2,1,0:T(8,128)S(1)} %get-tuple-element.18), channel_id=1, source_target_pairs={{0,16},{1,241},{2,18},{3,243},{4,20},{5,245},{6,22},{7,247},{8,24}... | collective-permute-start | bytes 835592 | tf_op jit(solution)/shard_map/ppermute | solution.py:216
  62.1 12.8 %collective-permute-start.5 = (f32[2,2,17,8,128]{4,3,2,1,0:T(8,128)S(1)}, f32[2,2,17,8,128]{4,3,2,1,0:T(8,128)S(1)}, u32[]{:S(2)}, u32[]{:S(2)}) collective-permute-start(f32[2,2,17,8,128]{4,3,2,1,0:T(8,128)S(1)} %get-tuple-element.19), channel_id=1, source_target_pairs={{0,240},{1,17},{2,242},{3,19},{4,244},{5,21},{6,246},{7,23},{8,248... | collective-permute-start | bytes 835592 | tf_op jit(solution)/shard_map/ppermute | solution.py:216
  65.0 9.9 %collective-permute-start.6 = (f32[1,2,17,8,128]{4,3,2,1,0:T(8,128)S(1)}, f32[1,2,17,8,128]{4,3,2,1,0:T(8,128)S(1)}, u32[]{:S(2)}, u32[]{:S(2)}) collective-permute-start(f32[1,2,17,8,128]{4,3,2,1,0:T(8,128)S(1)} %get-tuple-element.20), channel_id=1, source_target_pairs={{0,32},{1,225},{2,34},{3,227},{4,36},{5,229},{6,38},{7,231},{8,40}... | collective-permute-start | bytes 417800 | tf_op jit(solution)/shard_map/ppermute | solution.py:216
  78.1 8.4 %collective-permute-start.9 = (f32[8,16,1024]{2,1,0:T(8,128)S(1)}, f32[8,16,1024]{2,1,0:T(8,128)S(1)}, u32[]{:S(2)}, u32[]{:S(2)}) collective-permute-start(f32[8,16,1024]{2,1,0:T(8,128)S(1)} %get-tuple-element.28), channel_id=1, source_target_pairs={{0,1},{1,0},{2,3},{3,2},{4,5},{5,4},{6,7},{7,6},{8,9},{9,8},{10,11... | collective-permute-start | bytes 1572872 | tf_op jit(solution)/shard_map/ppermute | solution.py:198

commit v6 on v5

--- a/solution.py
+++ b/solution.py
@@ -89,6 +89,22 @@
         compiler_params=pltpu.CompilerParams(vmem_limit_bytes=16 * 1024 * 1024),
         cost_estimate=pl.CostEstimate(flops=8 * ab * width, bytes_accessed=8 * ab * width, transcendentals=0),
     )(labels_ab, labels_cd, w_slab)
+
+
+def gate_kernel(scal, block, out):
+    pass
+
+
+def after(scal, block):
+    vmem = pl.BlockSpec(memory_space=pltpu.VMEM)
+    return pl.pallas_call(
+        gate_kernel,
+        in_specs=[pl.BlockSpec(memory_space=pltpu.SMEM), vmem],
+        out_specs=vmem,
+        out_shape=jax.ShapeDtypeStruct(block.shape, block.dtype),
+        input_output_aliases={1: 0},
+        compiler_params=pltpu.CompilerParams(vmem_limit_bytes=2 * 1024 * 1024),
+    )(scal, block)
 
 
 def cut_kernel(picks, n_src, scal, *refs):
@@ -219,6 +235,7 @@
     x1 = move(own, 3)
     y1 = move(own, -3)
     scal, w_hi, w_lo = prepare(irrep_ab, irrep_cd, w_slab, n_vp)
+    x1 = after(scal, x1)
     x2 = move(x1, 3)
     y2 = move(y1, -3)
     to_x, to_y = cut(scal, [own, x1, y1], [(1, (0, 1, 2)), (2, (0, 1, 2))], win_tiles)

time: 111 us -> 111 us (level)
  starting transfers between devices: 51.6 us -> 49.2 us
  blocking collectives: 23.2 us -> 24.9 us
    ppermute x9, starting transfers between devices: 44.7 us -> 42.3 us  [move(): return lax.ppermute(array, ('vp', 'cd'), pairs)]
    all_to_all x1, blocking collectives: 23.2 us -> 24.9 us  [reduce_rows(): parts = lax.all_to_all(both, 'cd', 0, 0, axis_index_groups=groups)]
  transfers between devices with their start and end apart: 10 -> 10, of which waited for: 4 -> 6; matrix products, arithmetic and copies ran while one was open for 0% -> 0% of each run, Pallas kernels for 8% -> 9%
where the time goes in v6:
time: 111 us
  starting transfers between devices  49.2 us (44%)
  blocking collectives  24.9 us (22%)
  waiting for transfers between devices  18 us (16%)
  Pallas kernels  12.8 us (12%)
  local copies, waits for them, and re-layouts  4.93 us (4%)
    ppermute x9, starting transfers between devices, move(): return lax.ppermute(array, ('vp', 'cd'), pairs)  42.3 us
    all_to_all x1, blocking collectives, reduce_rows(): parts = lax.all_to_all(both, 'cd', 0, 0, axis_index_groups=groups)  24.9 us
    ppermute x9, waiting for transfers between devices, move(): return lax.ppermute(array, ('vp', 'cd'), pairs)  16.5 us
    pallas_call x2, Pallas kernels, contract(): pl.pallas_call(functools.partial(contract_kernel, rels, shapes, bool(old)...  7.79 us
    ppermute x1, starting transfers between devices, reduce_rows(): both = mine + lax.ppermute(other, 'cd', pair)  6.87 us
    unnamed x8, local copies, waits for them, and re-layouts  4.93 us
    pallas_call x1, Pallas kernels, prepare(): pl.pallas_call(functools.partial(prepare_kernel, owners, width // LANES +...  3.33 us
  transfers between devices with their start and end apart: 10, of which 6 were waited for; matrix products, arithmetic and copies ran while one was open for 0% of the time, Pallas kernels for 9%

profile of v6, /device:TPU:1, one launch (start us, length us, event | category | flops | bytes accessed | tf_op | source)
XLA Modules:
  0.0 110.7 jit_solution(8774086175334010982)
XLA Ops:
  0.0 18.7 %collective-permute-start = (f32[2,32,8,128]{3,2,1,0:T(8,128)}, f32[2,32,8,128]{3,2,1,0:T(8,128)S(1)}, u32[]{:S(2)}, u32[]{:S(2)}) collective-permute-start(f32[2,32,8,128]{3,2,1,0:T(8,128)} %bitcast.5), channel_id=1, source_target_pairs={{0,48},{1,209},{2,50},{3,211},{4,52},{5,213},{6,54},{7,215},{8,56}... | collective-permute-start | bytes 786440 | tf_op jit(solution)/shard_map/ppermute | solution.py:232
  18.7 1.9 %collective-permute-start.2 = (f32[2,32,8,128]{3,2,1,0:T(8,128)}, f32[2,32,8,128]{3,2,1,0:T(8,128)S(1)}, u32[]{:S(2)}, u32[]{:S(2)}) collective-permute-start(f32[2,32,8,128]{3,2,1,0:T(8,128)} %bitcast.6), channel_id=1, source_target_pairs={{0,208},{1,49},{2,210},{3,51},{4,212},{5,53},{6,214},{7,55},{8,216... | collective-permute-start | bytes 786440 | tf_op jit(solution)/shard_map/ppermute | solution.py:232
  20.7 0.0 copy-start
  20.7 3.4 %copy-done = f32[1024,2048]{1,0:T(8,128)S(1)} copy-done((f32[1024,2048]{1,0:T(8,128)S(1)}, f32[1024,2048]{1,0:T(8,128)}, u32[]{:S(2)}) %copy-start) | copy-done | bytes 8388632
  24.1 0.0 copy-start.2
  24.1 0.8 copy-done.2
  24.9 0.0 copy-start.3
  24.9 0.7 copy-done.3
  25.6 0.0 copy-start.1
  25.6 3.3 %shard_map.46 = (s32[16]{0:T(128)S(1)}, bf16[1024,2048]{1,0:T(8,128)(2,1)S(1)}, bf16[1024,2048]{1,0:T(8,128)(2,1)S(1)}) custom-call(s32[128,128]{1,0:T(8,128)S(1)} %bitcast.9, s32[32,128]{1,0:T(8,128)S(1)} %bitcast.10, f32[1024,2048]{1,0:T(8,128)S(1)} %copy-done), custom_call_target="tpu_custom_call" | custom-call | flops 16777216 | bytes 16777216 | tf_op jit(solution)/shard_map/pallas_call | solution.py:78
  29.0 6.1 %collective-permute-done.block = f32[2,32,8,128]{3,2,1,0:T(8,128)S(1)} collective-permute-done((f32[2,32,8,128]{3,2,1,0:T(8,128)}, f32[2,32,8,128]{3,2,1,0:T(8,128)S(1)}, u32[]{:S(2)}, u32[]{:S(2)}) %collective-permute-start) | collective-permute-done | bytes 262176 | tf_op jit(solution)/shard_map/ppermute | solution.py:232
  35.0 0.5 shard_map.47.refs_1_
  35.6 7.2 %collective-permute-start.1 = (f32[2,32,8,128]{3,2,1,0:T(8,128)S(1)}, f32[2,32,8,128]{3,2,1,0:T(8,128)S(1)}, u32[]{:S(2)}, u32[]{:S(2)}) collective-permute-start(f32[2,32,8,128]{3,2,1,0:T(8,128)S(1)} %shard_map.47.refs_1_), channel_id=1, source_target_pairs={{0,48},{1,209},{2,50},{3,211},{4,52},{5,213},{6,54},{7,215},{8,56}... | collective-permute-start | bytes 786440 | tf_op jit(solution)/shard_map/ppermute | solution.py:232
  42.8 0.0 collective-permute-done.2.refs_2_
  42.8 1.9 %collective-permute-start.3 = (f32[2,32,8,128]{3,2,1,0:T(8,128)S(1)}, f32[2,32,8,128]{3,2,1,0:T(8,128)S(1)}, u32[]{:S(2)}, u32[]{:S(2)}) collective-permute-start(f32[2,32,8,128]{3,2,1,0:T(8,128)S(1)} %collective-permute-done.2.refs_2_), channel_id=1, source_target_pairs={{0,208},{1,49},{2,210},{3,51},{4,212},{5,53},{6,214},{7,55},{8,216... | collective-permute-start | bytes 786440 | tf_op jit(solution)/shard_map/ppermute | solution.py:232
  44.7 0.0 copy-done.1
  44.7 0.6 shard_map.49
  45.3 1.9 %collective-permute-start.7 = (f32[3,2,17,8,128]{4,3,2,1,0:T(8,128)S(1)}, f32[3,2,17,8,128]{4,3,2,1,0:T(8,128)S(1)}, u32[]{:S(2)}, u32[]{:S(2)}) collective-permute-start(f32[3,2,17,8,128]{4,3,2,1,0:T(8,128)S(1)} %get-tuple-element.23), channel_id=1, source_target_pairs={{0,16},{1,241},{2,18},{3,243},{4,20},{5,245},{6,22},{7,247},{8,24}... | collective-permute-start | bytes 1253384 | tf_op jit(solution)/shard_map/ppermute | solution.py:232
  47.2 3.4 %collective-permute-start.8 = (f32[3,2,17,8,128]{4,3,2,1,0:T(8,128)S(1)}, f32[3,2,17,8,128]{4,3,2,1,0:T(8,128)S(1)}, u32[]{:S(2)}, u32[]{:S(2)}) collective-permute-start(f32[3,2,17,8,128]{4,3,2,1,0:T(8,128)S(1)} %get-tuple-element.24), channel_id=1, source_target_pairs={{0,240},{1,17},{2,242},{3,19},{4,244},{5,21},{6,246},{7,23},{8,248... | collective-permute-start | bytes 1253384 | tf_op jit(solution)/shard_map/ppermute | solution.py:232
  50.6 0.9 collective-permute-done.1.refs_0_.refs_3_
  51.5 8.4 %collective-permute-done.3.refs_1_.refs_4_ = f32[2,32,8,128]{3,2,1,0:T(8,128)S(1)} collective-permute-done((f32[2,32,8,128]{3,2,1,0:T(8,128)S(1)}, f32[2,32,8,128]{3,2,1,0:T(8,128)S(1)}, u32[]{:S(2)}, u32[]{:S(2)}) %collective-permute-start.3) | collective-permute-done | bytes 262176 | tf_op jit(solution)/shard_map/ppermute | solution.py:232
  59.9 0.6 shard_map.48
  60.5 1.9 %collective-permute-start.4 = (f32[2,2,17,8,128]{4,3,2,1,0:T(8,128)S(1)}, f32[2,2,17,8,128]{4,3,2,1,0:T(8,128)S(1)}, u32[]{:S(2)}, u32[]{:S(2)}) collective-permute-start(f32[2,2,17,8,128]{4,3,2,1,0:T(8,128)S(1)} %get-tuple-element.18), channel_id=1, source_target_pairs={{0,16},{1,241},{2,18},{3,243},{4,20},{5,245},{6,22},{7,247},{8,24}... | collective-permute-start | bytes 835592 | tf_op jit(solution)/shard_map/ppermute | solution.py:232
  62.4 3.4 %collective-permute-start.5 = (f32[2,2,17,8,128]{4,3,2,1,0:T(8,128)S(1)}, f32[2,2,17,8,128]{4,3,2,1,0:T(8,128)S(1)}, u32[]{:S(2)}, u32[]{:S(2)}) collective-permute-start(f32[2,2,17,8,128]{4,3,2,1,0:T(8,128)S(1)} %get-tuple-element.19), channel_id=1, source_target_pairs={{0,240},{1,17},{2,242},{3,19},{4,244},{5,21},{6,246},{7,23},{8,248... | collective-permute-start | bytes 835592 | tf_op jit(solution)/shard_map/ppermute | solution.py:232
  65.8 2.0 %collective-permute-start.6 = (f32[1,2,17,8,128]{4,3,2,1,0:T(8,128)S(1)}, f32[1,2,17,8,128]{4,3,2,1,0:T(8,128)S(1)}, u32[]{:S(2)}, u32[]{:S(2)}) collective-permute-start(f32[1,2,17,8,128]{4,3,2,1,0:T(8,128)S(1)} %get-tuple-element.20), channel_id=1, source_target_pairs={{0,32},{1,225},{2,34},{3,227},{4,36},{5,229},{6,38},{7,231},{8,40}... | collective-permute-start | bytes 417800 | tf_op jit(solution)/shard_map/ppermute | solution.py:232
  67.7 0.0 collective-permute-done.7.refs_5_
  67.8 0.0 collective-permute-done.8.refs_6_
  67.8 4.5 %shard_map.50 = (f32[8,16,1024]{2,1,0:T(8,128)S(1)}, f32[8,16,1024]{2,1,0:T(8,128)S(1)}) custom-call(s32[16]{0:T(128)S(1)} %get-tuple-element.17.scal, f32[2,32,8,128]{3,2,1,0:T(8,128)S(1)} %bitcast.8, f32[2,32,8,128]{3,2,1,0:T(8,128)S(1)} %shard_map.47.refs_1_, f32[2,32,8,128]{3,2,1,0:T(8,128)S(1)} %collective-permute-done.2.refs_2_, ...), custom_call_target="tpu_custom_call" | custom-call | flops 46137344 | bytes 2097152 | tf_op jit(solution)/shard_map/pallas_call | solution.py:197
  72.3 0.4 collective-permute-done.6.refs_2_
  72.8 0.0 collective-permute-done.4.refs_0_
  72.8 0.7 collective-permute-done.5.refs_1_
  73.5 3.2 %shard_map.51 = (f32[8,16,1024]{2,1,0:T(8,128)S(1)}, f32[8,16,1024]{2,1,0:T(8,128)S(1)}) custom-call(s32[16]{0:T(128)S(1)} %get-tuple-element.17.scal, f32[2,2,17,8,128]{4,3,2,1,0:T(8,128)S(1)} %collective-permute-done.4.refs_0_, f32[2,2,17,8,128]{4,3,2,1,0:T(8,128)S(1)} %collective-permute-done.5.refs_1_, ...), custom_call_target="tpu_custom_call", output_to_operand_aliasing={{0}: (6, {}), {1}: (7, {})} | custom-call | flops 20971520 | bytes 2097152 | tf_op jit(solution)/shard_map/pallas_call | solution.py:197
  76.8 6.9 %collective-permute-start.9 = (f32[8,16,1024]{2,1,0:T(8,128)S(1)}, f32[8,16,1024]{2,1,0:T(8,128)S(1)}, u32[]{:S(2)}, u32[]{:S(2)}) collective-permute-start(f32[8,16,1024]{2,1,0:T(8,128)S(1)} %get-tuple-element.28), channel_id=1, source_target_pairs={{0,1},{1,0},{2,3},{3,2},{4,5},{5,4},{6,7},{7,6},{8,9},{9,8},{10,11... | collective-permute-start | bytes 1572872 | tf_op jit(solution)/shard_map/ppermute | solution.py:214
  83.6 1.5 %collective-permute-done.9 = f32[8,16,1024]{2,1,0:T(8,128)S(1)} collective-permute-done((f32[8,16,1024]{2,1,0:T(8,128)S(1)}, f32[8,16,1024]{2,1,0:T(8,128)S(1)}, u32[]{:S(2)}, u32[]{:S(2)}) %collective-permute-start.9) | collective-permute-done | bytes 524320 | tf_op jit(solution)/shard_map/ppermute | solution.py:214
  85.1 0.1 add.3
  85.2 24.9 %all_to_all.5 = f32[8,16,1024]{2,1,0:T(8,128)S(1)} all-to-all(f32[8,16,1024]{2,1,0:T(8,128)S(1)} %add.3), channel_id=1, replica_groups={{0,2,4,6,8,10,12,14},{1,3,5,7,9,11,13,15},{16,18,20,22,24,26,28,30},{17..., dimensions={0} | all-to-all | bytes 1048576 | tf_op jit(solution)/shard_map/all_to_all | solution.py:216
  110.1 0.7 reduce_sum.9
Async XLA Ops:
  0.0 35.0 %collective-permute-start = (f32[2,32,8,128]{3,2,1,0:T(8,128)}, f32[2,32,8,128]{3,2,1,0:T(8,128)S(1)}, u32[]{:S(2)}, u32[]{:S(2)}) collective-permute-start(f32[2,32,8,128]{3,2,1,0:T(8,128)} %bitcast.5), channel_id=1, source_target_pairs={{0,48},{1,209},{2,50},{3,211},{4,52},{5,213},{6,54},{7,215},{8,56}... | collective-permute-start | bytes 786440 | tf_op jit(solution)/shard_map/ppermute | solution.py:232
  18.7 24.0 %collective-permute-start.2 = (f32[2,32,8,128]{3,2,1,0:T(8,128)}, f32[2,32,8,128]{3,2,1,0:T(8,128)S(1)}, u32[]{:S(2)}, u32[]{:S(2)}) collective-permute-start(f32[2,32,8,128]{3,2,1,0:T(8,128)} %bitcast.6), channel_id=1, source_target_pairs={{0,208},{1,49},{2,210},{3,51},{4,212},{5,53},{6,214},{7,55},{8,216... | collective-permute-start | bytes 786440 | tf_op jit(solution)/shard_map/ppermute | solution.py:232
  20.7 3.4 %copy-start = (f32[1024,2048]{1,0:T(8,128)S(1)}, f32[1024,2048]{1,0:T(8,128)}, u32[]{:S(2)}) copy-start(f32[1024,2048]{1,0:T(8,128)} %w_ref.1) | copy-start | bytes 25165828
  24.1 0.8 copy-start.2
  24.9 0.7 copy-start.3
  25.6 19.1 %copy-start.1 = (f32[16,4096]{1,0:T(8,128)S(1)}, f32[16,4096]{1,0:T(8,128)}, u32[]{:S(2)}) copy-start(f32[16,4096]{1,0:T(8,128)} %param.4) | copy-start | bytes 786436
  35.6 15.9 %collective-permute-start.1 = (f32[2,32,8,128]{3,2,1,0:T(8,128)S(1)}, f32[2,32,8,128]{3,2,1,0:T(8,128)S(1)}, u32[]{:S(2)}, u32[]{:S(2)}) collective-permute-start(f32[2,32,8,128]{3,2,1,0:T(8,128)S(1)} %shard_map.47.refs_1_), channel_id=1, source_target_pairs={{0,48},{1,209},{2,50},{3,211},{4,52},{5,213},{6,54},{7,215},{8,56}... | collective-permute-start | bytes 786440 | tf_op jit(solution)/shard_map/ppermute | solution.py:232
  42.8 17.1 %collective-permute-start.3 = (f32[2,32,8,128]{3,2,1,0:T(8,128)S(1)}, f32[2,32,8,128]{3,2,1,0:T(8,128)S(1)}, u32[]{:S(2)}, u32[]{:S(2)}) collective-permute-start(f32[2,32,8,128]{3,2,1,0:T(8,128)S(1)} %collective-permute-done.2.refs_2_), channel_id=1, source_target_pairs={{0,208},{1,49},{2,210},{3,51},{4,212},{5,53},{6,214},{7,55},{8,216... | collective-permute-start | bytes 786440 | tf_op jit(solution)/shard_map/ppermute | solution.py:232
  45.3 22.4 %collective-permute-start.7 = (f32[3,2,17,8,128]{4,3,2,1,0:T(8,128)S(1)}, f32[3,2,17,8,128]{4,3,2,1,0:T(8,128)S(1)}, u32[]{:S(2)}, u32[]{:S(2)}) collective-permute-start(f32[3,2,17,8,128]{4,3,2,1,0:T(8,128)S(1)} %get-tuple-element.23), channel_id=1, source_target_pairs={{0,16},{1,241},{2,18},{3,243},{4,20},{5,245},{6,22},{7,247},{8,24}... | collective-permute-start | bytes 1253384 | tf_op jit(solution)/shard_map/ppermute | solution.py:232
  47.2 20.5 %collective-permute-start.8 = (f32[3,2,17,8,128]{4,3,2,1,0:T(8,128)S(1)}, f32[3,2,17,8,128]{4,3,2,1,0:T(8,128)S(1)}, u32[]{:S(2)}, u32[]{:S(2)}) collective-permute-start(f32[3,2,17,8,128]{4,3,2,1,0:T(8,128)S(1)} %get-tuple-element.24), channel_id=1, source_target_pairs={{0,240},{1,17},{2,242},{3,19},{4,244},{5,21},{6,246},{7,23},{8,248... | collective-permute-start | bytes 1253384 | tf_op jit(solution)/shard_map/ppermute | solution.py:232
  60.5 12.3 %collective-permute-start.4 = (f32[2,2,17,8,128]{4,3,2,1,0:T(8,128)S(1)}, f32[2,2,17,8,128]{4,3,2,1,0:T(8,128)S(1)}, u32[]{:S(2)}, u32[]{:S(2)}) collective-permute-start(f32[2,2,17,8,128]{4,3,2,1,0:T(8,128)S(1)} %get-tuple-element.18), channel_id=1, source_target_pairs={{0,16},{1,241},{2,18},{3,243},{4,20},{5,245},{6,22},{7,247},{8,24}... | collective-permute-start | bytes 835592 | tf_op jit(solution)/shard_map/ppermute | solution.py:232
  62.4 11.1 %collective-permute-start.5 = (f32[2,2,17,8,128]{4,3,2,1,0:T(8,128)S(1)}, f32[2,2,17,8,128]{4,3,2,1,0:T(8,128)S(1)}, u32[]{:S(2)}, u32[]{:S(2)}) collective-permute-start(f32[2,2,17,8,128]{4,3,2,1,0:T(8,128)S(1)} %get-tuple-element.19), channel_id=1, source_target_pairs={{0,240},{1,17},{2,242},{3,19},{4,244},{5,21},{6,246},{7,23},{8,248... | collective-permute-start | bytes 835592 | tf_op jit(solution)/shard_map/ppermute | solution.py:232
  65.8 7.0 %collective-permute-start.6 = (f32[1,2,17,8,128]{4,3,2,1,0:T(8,128)S(1)}, f32[1,2,17,8,128]{4,3,2,1,0:T(8,128)S(1)}, u32[]{:S(2)}, u32[]{:S(2)}) collective-permute-start(f32[1,2,17,8,128]{4,3,2,1,0:T(8,128)S(1)} %get-tuple-element.20), channel_id=1, source_target_pairs={{0,32},{1,225},{2,34},{3,227},{4,36},{5,229},{6,38},{7,231},{8,40}... | collective-permute-start | bytes 417800 | tf_op jit(solution)/shard_map/ppermute | solution.py:232
  76.8 8.4 %collective-permute-start.9 = (f32[8,16,1024]{2,1,0:T(8,128)S(1)}, f32[8,16,1024]{2,1,0:T(8,128)S(1)}, u32[]{:S(2)}, u32[]{:S(2)}) collective-permute-start(f32[8,16,1024]{2,1,0:T(8,128)S(1)} %get-tuple-element.28), channel_id=1, source_target_pairs={{0,1},{1,0},{2,3},{3,2},{4,5},{5,4},{6,7},{7,6},{8,9},{9,8},{10,11... | collective-permute-start | bytes 1572872 | tf_op jit(solution)/shard_map/ppermute | solution.py:214
